TPU v7x, 128 devices: a whole 4x4x4 slice. The times are simulated.
128 devices in a mesh: sample: 32 (over x, y, core), axial: 4 (over z).
Axes of the slice: x: 4, y: 4, z: 4, core: 2. Of those that a mesh axis runs over, the one named last changes fastest.
Arguments:
- pair: bfloat16 [32, 256, 256, 128], P('sample', 'axial'), may hold values from -6 to 6
- lengths: int32 [32], replicated, may hold values from 85 to 256, as said below
- block_group: int32 [32, 32], replicated, may hold values from 0 to 31, as said below
- w_proj: bfloat16 [128, 512], replicated
- w_bias: bfloat16 [128, 4], replicated
- w_out: bfloat16 [128, 128], replicated, may hold values from -1.5 to 1.5
- w_up: bfloat16 [128, 512], replicated, may hold values from -0.5 to 0.5
- w_down: bfloat16 [512, 128], replicated, may hold values from -0.25 to 0.25
Outputs:
- pair_out: bfloat16 [32, 4, 32, 2, 256, 128], P('sample', 'axial')
Inputs may be any that keep to these rules, and one draw needn't show every extreme that they name: lengths run from 85 to 256; some crop has exactly 256 residues. Each row and each column of block_group names every group once.
All inputs are finite; a program needn't handle non-finite values.
Results may differ from a plain program's by a relative error of at most 0.0085.
Values may be sent and summed in bfloat16 or wider, within the bound.
No kernel may reach another device: no remote copies, remote signals or barrier semaphores. Data moves between devices by JAX's collectives and lax.ppermute only.
A program may use at most 128 MiB of HBM per device.

v0:
```python
import jax
import jax.numpy as jnp
from jax import lax
from jax.sharding import PartitionSpec as P


def layer_norm(values_in):
    values_in = values_in.astype(jnp.float32)
    centre = values_in - jnp.mean(values_in, -1, keepdims=True)
    spread = jnp.mean(centre * centre, -1, keepdims=True)
    return centre * lax.rsqrt(spread + 1e-05)


def attend(normed, bias, key_live, w_proj, w_out):
    groups, rows, width_l, chans = normed.shape
    heads = bias.shape[1]
    inner = w_proj.shape[1] // 4
    size_h = inner // heads
    f32 = jnp.float32
    bf16 = jnp.bfloat16
    projected = jnp.einsum("grlc,cf->grlf", normed, w_proj, preferred_element_type=f32)
    shape_h = (groups, rows, width_l, heads, size_h)
    query = (projected[..., :inner] * size_h ** (-0.5)).astype(bf16).reshape(shape_h)
    keys = projected[..., inner : 2 * inner].astype(bf16).reshape(shape_h)
    values = projected[..., 2 * inner : 3 * inner].astype(bf16).reshape(shape_h)
    gate = jax.nn.sigmoid(projected[..., 3 * inner :])
    scores = jnp.einsum("grjhd,grkhd->grhjk", query, keys, preferred_element_type=f32) + bias[
        :, None
    ].astype(f32)
    scores = jnp.where(key_live[:, None, None, None, :], scores, -1000000000.0)
    weights = jax.nn.softmax(scores, axis=-1).astype(bf16)
    attended = jnp.einsum(
        "grhjk,grkhd->grjhd", weights, values, preferred_element_type=f32
    ).reshape(groups, rows, width_l, inner)
    gated = (gate * attended).astype(bf16)
    return jnp.einsum("grlf,fc->grlc", gated, w_out, preferred_element_type=f32)


def update_rows(block, normed, bias, row_ids, length, w_proj, w_out, w_up, w_down):
    width_l = block.shape[2]
    f32 = jnp.float32
    bf16 = jnp.bfloat16
    columns = jnp.arange(width_l, dtype=jnp.int32)
    key_live = columns[None, :] < length[:, None]
    pair_live = (row_ids < length[:, None])[:, :, None] & key_live[:, None, :]
    update = lax.cond(
        jnp.any(pair_live),
        lambda: attend(normed, bias, key_live, w_proj, w_out),
        lambda: jnp.zeros(block.shape, f32),
    )
    middle = (block.astype(f32) + jnp.where(pair_live[..., None], update, 0.0)).astype(bf16)
    middle = lax.optimization_barrier(middle)
    normed_mid = layer_norm(middle).astype(bf16)
    hidden = jax.nn.relu(
        jnp.einsum("grlc,cf->grlf", normed_mid, w_up, preferred_element_type=f32)
    ).astype(bf16)
    down = jnp.einsum("grlf,fc->grlc", hidden, w_down, preferred_element_type=f32)
    return (middle.astype(f32) + down).astype(bf16)


def shards(pair, lengths, block_group, w_proj, w_bias, w_out, w_up, w_down):
    group_idx = lax.axis_index("sample")
    axial_idx = lax.axis_index("axial")
    groups_n = lax.axis_size("sample")
    ax_rows = pair.shape[1]
    width_l = pair.shape[2]
    chans = pair.shape[3]
    blk_rows = ax_rows // groups_n
    local = pair[0]
    normed = layer_norm(local).astype(jnp.bfloat16)
    bias_local = jnp.einsum(
        "ilc,ch->hil", normed, w_bias, preferred_element_type=jnp.float32
    ).astype(jnp.bfloat16)
    group_ids = jnp.arange(groups_n, dtype=jnp.int32)
    own_row = jnp.take(block_group, group_idx, axis=0)
    send_order = jnp.sum(
        jnp.where(own_row[None, :] == group_ids[:, None], group_ids[None, :], 0), 1
    )
    crop_bias = lax.all_gather(bias_local, "axial", axis=1, tiled=True)
    length = jnp.take(lengths, group_idx)
    blocks = local.reshape(ax_rows // 4, 1, 4, width_l, chans)
    normeds = normed.reshape(ax_rows // 4, 1, 4, width_l, chans)
    row_ids = (axial_idx * ax_rows + jnp.arange(ax_rows, dtype=jnp.int32)).reshape(
        ax_rows // 4, 1, 4
    )

    def home_step(item):
        return update_rows(
            item[0], item[1], crop_bias[None], item[2], length[None], w_proj, w_out, w_up, w_down
        )

    updated = lax.map(home_step, (blocks, normeds, row_ids))
    shuffled = jnp.take(updated.reshape(groups_n, blk_rows, width_l, chans), send_order, axis=0)
    arrived = lax.all_to_all(shuffled, "sample", split_axis=0, concat_axis=0, tiled=True)
    return arrived.reshape(1, 1, groups_n, blk_rows, width_l, chans)


def solution(mesh):
    return jax.shard_map(
        shards,
        mesh=mesh,
        in_specs=(P("sample", "axial", None, None), P(), P(), P(), P(), P(), P(), P()),
        out_specs=P("sample", "axial", None, None, None, None),
        check_vma=False,
    )
```

profile of v0, /device:TPU:1, one launch (start us, length us, event | category | flops | bytes accessed | tf_op | source)
XLA Modules:
  0.0 442.2 jit_solution(13899952686286076652)
XLA Ops:
  0.0 3.5 convert_reduce_fusion.1
  3.5 4.8 %fusion.49 = f32[64,256]{1,0:T(8,128)S(1)} fusion(bf16[1,64,256,128]{3,2,1,0:T(8,128)(2,1)S(1)} %copy-done.1, f32[64,256]{1,0:T(8,128)S(1)} %broadcast_multiply_fusion.1), kind=kLoop, calls=%fused_computation.64 | loop fusion | flops 8372224 | bytes 4325376 | tf_op jit(solution)/shard_map/reduce_sum | solution.py:10
  10.8 6.3 %fusion.58 = bf16[4,64,256]{2,0,1:T(4,128)(2,1)S(1)} fusion(bf16[1,64,256,128]{3,2,1,0:T(8,128)(2,1)} %param.12, f32[64,256]{1,0:T(8,128)S(1)} %add_rsqrt_fusion.1, f32[64,256]{1,0:T(8,128)S(1)} %broadcast_multiply_fusion.1, bf16[128,4]{0,1:T(4,128)(2,1)S(1)} %copy-done), kind=kOutput, calls=%fused_computation.72 | convolution fusion | flops 25231360 | bytes 4457472 | tf_op jit(solution)/shard_map/ilc,ch->hil/dot_general | solution.py:71
  17.1 13.4 %all_gather.3 = bf16[4,256,256]{2,0,1:T(4,128)(2,1)S(1)} all-gather(bf16[4,64,256]{2,0,1:T(4,128)(2,1)S(1)} %fusion.58), channel_id=1, replica_groups=mesh['sample'=32,'axial'=4] {'axial'}, dimensions={1}, use_global_device_ids=true | all-gather | bytes 655360 | tf_op jit(solution)/shard_map/all_gather | solution.py:79
  32.0 8.8 %multiply_convert_fusion = bf16[16,1,4,256,128]{4,3,2,1,0:T(8,128)(2,1)} fusion(bf16[16,1,4,256,128]{4,3,2,1,0:T(8,128)(2,1)} %bitcast.109, f32[16,4,256]{2,1,0:T(4,128)S(1)} %rsqrt.21, f32[16,4,256]{2,1,0:T(4,128)S(1)} %div.29), kind=kLoop, calls=%fused_computation.66 | loop fusion | flops 8388608 | bytes 8519680 | tf_op jit(solution)/shard_map/convert_element_type | solution.py:70
  40.8 331.3 %while.12 = (s32[]{:T(128)}, bf16[16,1,4,256,128]{4,3,2,1,0:T(8,128)(2,1)}, bf16[16,1,4,256,128]{4,3,2,1,0:T(8,128)(2,1)}, s32[16,1,4]{2,1,0:T(1,128)}, s32[]{:T...) while((s32[]{:T(128)}, ...), condition=%wide.region_11.12_spmd, body=%wide.region_3.11_spmd.sunk | while | flops 581702400 | bytes 24619500 | solution.py:92
  42.8 14.5 %conditional.2 = (f32[1,4,256,128]{3,2,1,0:T(8,128)S(1)}) conditional(s32[]{:T(128)} %convert_element_type.188, () %tuple.45, (bf16[16,1,4,256,128]{4,3,2,1,0:T(8,128)(2,1)}, s32[]{:T(128)}, bf16[128,512]{1,0:T(8,128)(2,1)S(1)}, s32[]{:T(128)}, s32[1,256]{1,0:T(1,128)S(1)}, /*index=5*/bf16[4,256,256]{1,2,0:T(8,128)(2,1)S(1)}, ...), branch_computations={%region_5.5_spmd, %region_6.8_spmd} | conditional | flops 309985792 | bytes 21956620 | solution.py:46
  46.6 5.5 %fusion.66 = (f32[4,4,256]{2,1,0:T(4,128)}, f32[4,4,256,256]{2,3,1,0:T(8,128)}) fusion(f32[4,256,256]{1,2,0:T(8,128)} %convert_element_type.71, pred[256]{0:T(512)(128)(4,1)S(1)} %compare_reduce_fusion, bf16[4,256,4,32]{1,3,2,0:T(8,128)(2,1)} %bitcast.114, bf16[4,256,4,32]{1,3,2,0:T(8,128)(2,1)S(1)} %bitcast.113), kind=kOutput, calls=%fused_computation.88 | convolution fusion | flops 71303424 | bytes 5783808 | tf_op jit(solution)/shard_map/while/body/eval_jaxpr/cond/branch_1_fun/sub | solution.py:31
  63.6 14.5 %conditional.2 = (f32[1,4,256,128]{3,2,1,0:T(8,128)S(1)}) conditional(s32[]{:T(128)} %convert_element_type.188, () %tuple.45, (bf16[16,1,4,256,128]{4,3,2,1,0:T(8,128)(2,1)}, s32[]{:T(128)}, bf16[128,512]{1,0:T(8,128)(2,1)S(1)}, s32[]{:T(128)}, s32[1,256]{1,0:T(1,128)S(1)}, /*index=5*/bf16[4,256,256]{1,2,0:T(8,128)(2,1)S(1)}, ...), branch_computations={%region_5.5_spmd, %region_6.8_spmd} | conditional | flops 309985792 | bytes 21956620 | solution.py:46
  67.3 5.6 %fusion.66 = (f32[4,4,256]{2,1,0:T(4,128)}, f32[4,4,256,256]{2,3,1,0:T(8,128)}) fusion(f32[4,256,256]{1,2,0:T(8,128)} %convert_element_type.71, pred[256]{0:T(512)(128)(4,1)S(1)} %compare_reduce_fusion, bf16[4,256,4,32]{1,3,2,0:T(8,128)(2,1)} %bitcast.114, bf16[4,256,4,32]{1,3,2,0:T(8,128)(2,1)S(1)} %bitcast.113), kind=kOutput, calls=%fused_computation.88 | convolution fusion | flops 71303424 | bytes 5783808 | tf_op jit(solution)/shard_map/while/body/eval_jaxpr/cond/branch_1_fun/sub | solution.py:31
  73.1 2.7 fusion.5
  84.2 14.5 %conditional.2 = (f32[1,4,256,128]{3,2,1,0:T(8,128)S(1)}) conditional(s32[]{:T(128)} %convert_element_type.188, () %tuple.45, (bf16[16,1,4,256,128]{4,3,2,1,0:T(8,128)(2,1)}, s32[]{:T(128)}, bf16[128,512]{1,0:T(8,128)(2,1)S(1)}, s32[]{:T(128)}, s32[1,256]{1,0:T(1,128)S(1)}, /*index=5*/bf16[4,256,256]{1,2,0:T(8,128)(2,1)S(1)}, ...), branch_computations={%region_5.5_spmd, %region_6.8_spmd} | conditional | flops 309985792 | bytes 21956620 | solution.py:46
  88.0 5.6 %fusion.66 = (f32[4,4,256]{2,1,0:T(4,128)}, f32[4,4,256,256]{2,3,1,0:T(8,128)}) fusion(f32[4,256,256]{1,2,0:T(8,128)} %convert_element_type.71, pred[256]{0:T(512)(128)(4,1)S(1)} %compare_reduce_fusion, bf16[4,256,4,32]{1,3,2,0:T(8,128)(2,1)} %bitcast.114, bf16[4,256,4,32]{1,3,2,0:T(8,128)(2,1)S(1)} %bitcast.113), kind=kOutput, calls=%fused_computation.88 | convolution fusion | flops 71303424 | bytes 5783808 | tf_op jit(solution)/shard_map/while/body/eval_jaxpr/cond/branch_1_fun/sub | solution.py:31
  93.7 2.7 fusion.5
  105.0 14.5 %conditional.2 = (f32[1,4,256,128]{3,2,1,0:T(8,128)S(1)}) conditional(s32[]{:T(128)} %convert_element_type.188, () %tuple.45, (bf16[16,1,4,256,128]{4,3,2,1,0:T(8,128)(2,1)}, s32[]{:T(128)}, bf16[128,512]{1,0:T(8,128)(2,1)S(1)}, s32[]{:T(128)}, s32[1,256]{1,0:T(1,128)S(1)}, /*index=5*/bf16[4,256,256]{1,2,0:T(8,128)(2,1)S(1)}, ...), branch_computations={%region_5.5_spmd, %region_6.8_spmd} | conditional | flops 309985792 | bytes 21956620 | solution.py:46
  108.8 5.6 %fusion.66 = (f32[4,4,256]{2,1,0:T(4,128)}, f32[4,4,256,256]{2,3,1,0:T(8,128)}) fusion(f32[4,256,256]{1,2,0:T(8,128)} %convert_element_type.71, pred[256]{0:T(512)(128)(4,1)S(1)} %compare_reduce_fusion, bf16[4,256,4,32]{1,3,2,0:T(8,128)(2,1)} %bitcast.114, bf16[4,256,4,32]{1,3,2,0:T(8,128)(2,1)S(1)} %bitcast.113), kind=kOutput, calls=%fused_computation.88 | convolution fusion | flops 71303424 | bytes 5783808 | tf_op jit(solution)/shard_map/while/body/eval_jaxpr/cond/branch_1_fun/sub | solution.py:31
  125.7 14.5 %conditional.2 = (f32[1,4,256,128]{3,2,1,0:T(8,128)S(1)}) conditional(s32[]{:T(128)} %convert_element_type.188, () %tuple.45, (bf16[16,1,4,256,128]{4,3,2,1,0:T(8,128)(2,1)}, s32[]{:T(128)}, bf16[128,512]{1,0:T(8,128)(2,1)S(1)}, s32[]{:T(128)}, s32[1,256]{1,0:T(1,128)S(1)}, /*index=5*/bf16[4,256,256]{1,2,0:T(8,128)(2,1)S(1)}, ...), branch_computations={%region_5.5_spmd, %region_6.8_spmd} | conditional | flops 309985792 | bytes 21956620 | solution.py:46
  129.5 5.6 %fusion.66 = (f32[4,4,256]{2,1,0:T(4,128)}, f32[4,4,256,256]{2,3,1,0:T(8,128)}) fusion(f32[4,256,256]{1,2,0:T(8,128)} %convert_element_type.71, pred[256]{0:T(512)(128)(4,1)S(1)} %compare_reduce_fusion, bf16[4,256,4,32]{1,3,2,0:T(8,128)(2,1)} %bitcast.114, bf16[4,256,4,32]{1,3,2,0:T(8,128)(2,1)S(1)} %bitcast.113), kind=kOutput, calls=%fused_computation.88 | convolution fusion | flops 71303424 | bytes 5783808 | tf_op jit(solution)/shard_map/while/body/eval_jaxpr/cond/branch_1_fun/sub | solution.py:31
  135.2 2.7 fusion.5
  146.4 14.5 %conditional.2 = (f32[1,4,256,128]{3,2,1,0:T(8,128)S(1)}) conditional(s32[]{:T(128)} %convert_element_type.188, () %tuple.45, (bf16[16,1,4,256,128]{4,3,2,1,0:T(8,128)(2,1)}, s32[]{:T(128)}, bf16[128,512]{1,0:T(8,128)(2,1)S(1)}, s32[]{:T(128)}, s32[1,256]{1,0:T(1,128)S(1)}, /*index=5*/bf16[4,256,256]{1,2,0:T(8,128)(2,1)S(1)}, ...), branch_computations={%region_5.5_spmd, %region_6.8_spmd} | conditional | flops 309985792 | bytes 21956620 | solution.py:46
  150.2 5.6 %fusion.66 = (f32[4,4,256]{2,1,0:T(4,128)}, f32[4,4,256,256]{2,3,1,0:T(8,128)}) fusion(f32[4,256,256]{1,2,0:T(8,128)} %convert_element_type.71, pred[256]{0:T(512)(128)(4,1)S(1)} %compare_reduce_fusion, bf16[4,256,4,32]{1,3,2,0:T(8,128)(2,1)} %bitcast.114, bf16[4,256,4,32]{1,3,2,0:T(8,128)(2,1)S(1)} %bitcast.113), kind=kOutput, calls=%fused_computation.88 | convolution fusion | flops 71303424 | bytes 5783808 | tf_op jit(solution)/shard_map/while/body/eval_jaxpr/cond/branch_1_fun/sub | solution.py:31
  155.9 2.7 fusion.5
  167.1 14.5 %conditional.2 = (f32[1,4,256,128]{3,2,1,0:T(8,128)S(1)}) conditional(s32[]{:T(128)} %convert_element_type.188, () %tuple.45, (bf16[16,1,4,256,128]{4,3,2,1,0:T(8,128)(2,1)}, s32[]{:T(128)}, bf16[128,512]{1,0:T(8,128)(2,1)S(1)}, s32[]{:T(128)}, s32[1,256]{1,0:T(1,128)S(1)}, /*index=5*/bf16[4,256,256]{1,2,0:T(8,128)(2,1)S(1)}, ...), branch_computations={%region_5.5_spmd, %region_6.8_spmd} | conditional | flops 309985792 | bytes 21956620 | solution.py:46
  170.9 5.5 %fusion.66 = (f32[4,4,256]{2,1,0:T(4,128)}, f32[4,4,256,256]{2,3,1,0:T(8,128)}) fusion(f32[4,256,256]{1,2,0:T(8,128)} %convert_element_type.71, pred[256]{0:T(512)(128)(4,1)S(1)} %compare_reduce_fusion, bf16[4,256,4,32]{1,3,2,0:T(8,128)(2,1)} %bitcast.114, bf16[4,256,4,32]{1,3,2,0:T(8,128)(2,1)S(1)} %bitcast.113), kind=kOutput, calls=%fused_computation.88 | convolution fusion | flops 71303424 | bytes 5783808 | tf_op jit(solution)/shard_map/while/body/eval_jaxpr/cond/branch_1_fun/sub | solution.py:31
  187.7 14.5 %conditional.2 = (f32[1,4,256,128]{3,2,1,0:T(8,128)S(1)}) conditional(s32[]{:T(128)} %convert_element_type.188, () %tuple.45, (bf16[16,1,4,256,128]{4,3,2,1,0:T(8,128)(2,1)}, s32[]{:T(128)}, bf16[128,512]{1,0:T(8,128)(2,1)S(1)}, s32[]{:T(128)}, s32[1,256]{1,0:T(1,128)S(1)}, /*index=5*/bf16[4,256,256]{1,2,0:T(8,128)(2,1)S(1)}, ...), branch_computations={%region_5.5_spmd, %region_6.8_spmd} | conditional | flops 309985792 | bytes 21956620 | solution.py:46
  191.5 5.6 %fusion.66 = (f32[4,4,256]{2,1,0:T(4,128)}, f32[4,4,256,256]{2,3,1,0:T(8,128)}) fusion(f32[4,256,256]{1,2,0:T(8,128)} %convert_element_type.71, pred[256]{0:T(512)(128)(4,1)S(1)} %compare_reduce_fusion, bf16[4,256,4,32]{1,3,2,0:T(8,128)(2,1)} %bitcast.114, bf16[4,256,4,32]{1,3,2,0:T(8,128)(2,1)S(1)} %bitcast.113), kind=kOutput, calls=%fused_computation.88 | convolution fusion | flops 71303424 | bytes 5783808 | tf_op jit(solution)/shard_map/while/body/eval_jaxpr/cond/branch_1_fun/sub | solution.py:31
  197.2 2.7 fusion.5
  208.4 14.5 %conditional.2 = (f32[1,4,256,128]{3,2,1,0:T(8,128)S(1)}) conditional(s32[]{:T(128)} %convert_element_type.188, () %tuple.45, (bf16[16,1,4,256,128]{4,3,2,1,0:T(8,128)(2,1)}, s32[]{:T(128)}, bf16[128,512]{1,0:T(8,128)(2,1)S(1)}, s32[]{:T(128)}, s32[1,256]{1,0:T(1,128)S(1)}, /*index=5*/bf16[4,256,256]{1,2,0:T(8,128)(2,1)S(1)}, ...), branch_computations={%region_5.5_spmd, %region_6.8_spmd} | conditional | flops 309985792 | bytes 21956620 | solution.py:46
  212.2 5.5 %fusion.66 = (f32[4,4,256]{2,1,0:T(4,128)}, f32[4,4,256,256]{2,3,1,0:T(8,128)}) fusion(f32[4,256,256]{1,2,0:T(8,128)} %convert_element_type.71, pred[256]{0:T(512)(128)(4,1)S(1)} %compare_reduce_fusion, bf16[4,256,4,32]{1,3,2,0:T(8,128)(2,1)} %bitcast.114, bf16[4,256,4,32]{1,3,2,0:T(8,128)(2,1)S(1)} %bitcast.113), kind=kOutput, calls=%fused_computation.88 | convolution fusion | flops 71303424 | bytes 5783808 | tf_op jit(solution)/shard_map/while/body/eval_jaxpr/cond/branch_1_fun/sub | solution.py:31
  229.1 14.5 %conditional.2 = (f32[1,4,256,128]{3,2,1,0:T(8,128)S(1)}) conditional(s32[]{:T(128)} %convert_element_type.188, () %tuple.45, (bf16[16,1,4,256,128]{4,3,2,1,0:T(8,128)(2,1)}, s32[]{:T(128)}, bf16[128,512]{1,0:T(8,128)(2,1)S(1)}, s32[]{:T(128)}, s32[1,256]{1,0:T(1,128)S(1)}, /*index=5*/bf16[4,256,256]{1,2,0:T(8,128)(2,1)S(1)}, ...), branch_computations={%region_5.5_spmd, %region_6.8_spmd} | conditional | flops 309985792 | bytes 21956620 | solution.py:46
  232.9 5.6 %fusion.66 = (f32[4,4,256]{2,1,0:T(4,128)}, f32[4,4,256,256]{2,3,1,0:T(8,128)}) fusion(f32[4,256,256]{1,2,0:T(8,128)} %convert_element_type.71, pred[256]{0:T(512)(128)(4,1)S(1)} %compare_reduce_fusion, bf16[4,256,4,32]{1,3,2,0:T(8,128)(2,1)} %bitcast.114, bf16[4,256,4,32]{1,3,2,0:T(8,128)(2,1)S(1)} %bitcast.113), kind=kOutput, calls=%fused_computation.88 | convolution fusion | flops 71303424 | bytes 5783808 | tf_op jit(solution)/shard_map/while/body/eval_jaxpr/cond/branch_1_fun/sub | solution.py:31
  238.6 2.7 fusion.5
  249.9 14.5 %conditional.2 = (f32[1,4,256,128]{3,2,1,0:T(8,128)S(1)}) conditional(s32[]{:T(128)} %convert_element_type.188, () %tuple.45, (bf16[16,1,4,256,128]{4,3,2,1,0:T(8,128)(2,1)}, s32[]{:T(128)}, bf16[128,512]{1,0:T(8,128)(2,1)S(1)}, s32[]{:T(128)}, s32[1,256]{1,0:T(1,128)S(1)}, /*index=5*/bf16[4,256,256]{1,2,0:T(8,128)(2,1)S(1)}, ...), branch_computations={%region_5.5_spmd, %region_6.8_spmd} | conditional | flops 309985792 | bytes 21956620 | solution.py:46
  253.6 5.5 %fusion.66 = (f32[4,4,256]{2,1,0:T(4,128)}, f32[4,4,256,256]{2,3,1,0:T(8,128)}) fusion(f32[4,256,256]{1,2,0:T(8,128)} %convert_element_type.71, pred[256]{0:T(512)(128)(4,1)S(1)} %compare_reduce_fusion, bf16[4,256,4,32]{1,3,2,0:T(8,128)(2,1)} %bitcast.114, bf16[4,256,4,32]{1,3,2,0:T(8,128)(2,1)S(1)} %bitcast.113), kind=kOutput, calls=%fused_computation.88 | convolution fusion | flops 71303424 | bytes 5783808 | tf_op jit(solution)/shard_map/while/body/eval_jaxpr/cond/branch_1_fun/sub | solution.py:31
  270.6 14.5 %conditional.2 = (f32[1,4,256,128]{3,2,1,0:T(8,128)S(1)}) conditional(s32[]{:T(128)} %convert_element_type.188, () %tuple.45, (bf16[16,1,4,256,128]{4,3,2,1,0:T(8,128)(2,1)}, s32[]{:T(128)}, bf16[128,512]{1,0:T(8,128)(2,1)S(1)}, s32[]{:T(128)}, s32[1,256]{1,0:T(1,128)S(1)}, /*index=5*/bf16[4,256,256]{1,2,0:T(8,128)(2,1)S(1)}, ...), branch_computations={%region_5.5_spmd, %region_6.8_spmd} | conditional | flops 309985792 | bytes 21956620 | solution.py:46
  274.4 5.5 %fusion.66 = (f32[4,4,256]{2,1,0:T(4,128)}, f32[4,4,256,256]{2,3,1,0:T(8,128)}) fusion(f32[4,256,256]{1,2,0:T(8,128)} %convert_element_type.71, pred[256]{0:T(512)(128)(4,1)S(1)} %compare_reduce_fusion, bf16[4,256,4,32]{1,3,2,0:T(8,128)(2,1)} %bitcast.114, bf16[4,256,4,32]{1,3,2,0:T(8,128)(2,1)S(1)} %bitcast.113), kind=kOutput, calls=%fused_computation.88 | convolution fusion | flops 71303424 | bytes 5783808 | tf_op jit(solution)/shard_map/while/body/eval_jaxpr/cond/branch_1_fun/sub | solution.py:31
  291.3 14.5 %conditional.2 = (f32[1,4,256,128]{3,2,1,0:T(8,128)S(1)}) conditional(s32[]{:T(128)} %convert_element_type.188, () %tuple.45, (bf16[16,1,4,256,128]{4,3,2,1,0:T(8,128)(2,1)}, s32[]{:T(128)}, bf16[128,512]{1,0:T(8,128)(2,1)S(1)}, s32[]{:T(128)}, s32[1,256]{1,0:T(1,128)S(1)}, /*index=5*/bf16[4,256,256]{1,2,0:T(8,128)(2,1)S(1)}, ...), branch_computations={%region_5.5_spmd, %region_6.8_spmd} | conditional | flops 309985792 | bytes 21956620 | solution.py:46
  295.1 5.6 %fusion.66 = (f32[4,4,256]{2,1,0:T(4,128)}, f32[4,4,256,256]{2,3,1,0:T(8,128)}) fusion(f32[4,256,256]{1,2,0:T(8,128)} %convert_element_type.71, pred[256]{0:T(512)(128)(4,1)S(1)} %compare_reduce_fusion, bf16[4,256,4,32]{1,3,2,0:T(8,128)(2,1)} %bitcast.114, bf16[4,256,4,32]{1,3,2,0:T(8,128)(2,1)S(1)} %bitcast.113), kind=kOutput, calls=%fused_computation.88 | convolution fusion | flops 71303424 | bytes 5783808 | tf_op jit(solution)/shard_map/while/body/eval_jaxpr/cond/branch_1_fun/sub | solution.py:31
  300.8 2.7 fusion.5
  311.9 14.5 %conditional.2 = (f32[1,4,256,128]{3,2,1,0:T(8,128)S(1)}) conditional(s32[]{:T(128)} %convert_element_type.188, () %tuple.45, (bf16[16,1,4,256,128]{4,3,2,1,0:T(8,128)(2,1)}, s32[]{:T(128)}, bf16[128,512]{1,0:T(8,128)(2,1)S(1)}, s32[]{:T(128)}, s32[1,256]{1,0:T(1,128)S(1)}, /*index=5*/bf16[4,256,256]{1,2,0:T(8,128)(2,1)S(1)}, ...), branch_computations={%region_5.5_spmd, %region_6.8_spmd} | conditional | flops 309985792 | bytes 21956620 | solution.py:46
  315.7 5.6 %fusion.66 = (f32[4,4,256]{2,1,0:T(4,128)}, f32[4,4,256,256]{2,3,1,0:T(8,128)}) fusion(f32[4,256,256]{1,2,0:T(8,128)} %convert_element_type.71, pred[256]{0:T(512)(128)(4,1)S(1)} %compare_reduce_fusion, bf16[4,256,4,32]{1,3,2,0:T(8,128)(2,1)} %bitcast.114, bf16[4,256,4,32]{1,3,2,0:T(8,128)(2,1)S(1)} %bitcast.113), kind=kOutput, calls=%fused_computation.88 | convolution fusion | flops 71303424 | bytes 5783808 | tf_op jit(solution)/shard_map/while/body/eval_jaxpr/cond/branch_1_fun/sub | solution.py:31
  332.6 14.5 %conditional.2 = (f32[1,4,256,128]{3,2,1,0:T(8,128)S(1)}) conditional(s32[]{:T(128)} %convert_element_type.188, () %tuple.45, (bf16[16,1,4,256,128]{4,3,2,1,0:T(8,128)(2,1)}, s32[]{:T(128)}, bf16[128,512]{1,0:T(8,128)(2,1)S(1)}, s32[]{:T(128)}, s32[1,256]{1,0:T(1,128)S(1)}, /*index=5*/bf16[4,256,256]{1,2,0:T(8,128)(2,1)S(1)}, ...), branch_computations={%region_5.5_spmd, %region_6.8_spmd} | conditional | flops 309985792 | bytes 21956620 | solution.py:46
  336.4 5.6 %fusion.66 = (f32[4,4,256]{2,1,0:T(4,128)}, f32[4,4,256,256]{2,3,1,0:T(8,128)}) fusion(f32[4,256,256]{1,2,0:T(8,128)} %convert_element_type.71, pred[256]{0:T(512)(128)(4,1)S(1)} %compare_reduce_fusion, bf16[4,256,4,32]{1,3,2,0:T(8,128)(2,1)} %bitcast.114, bf16[4,256,4,32]{1,3,2,0:T(8,128)(2,1)S(1)} %bitcast.113), kind=kOutput, calls=%fused_computation.88 | convolution fusion | flops 71303424 | bytes 5783808 | tf_op jit(solution)/shard_map/while/body/eval_jaxpr/cond/branch_1_fun/sub | solution.py:31
  353.4 14.5 %conditional.2 = (f32[1,4,256,128]{3,2,1,0:T(8,128)S(1)}) conditional(s32[]{:T(128)} %convert_element_type.188, () %tuple.45, (bf16[16,1,4,256,128]{4,3,2,1,0:T(8,128)(2,1)}, s32[]{:T(128)}, bf16[128,512]{1,0:T(8,128)(2,1)S(1)}, s32[]{:T(128)}, s32[1,256]{1,0:T(1,128)S(1)}, /*index=5*/bf16[4,256,256]{1,2,0:T(8,128)(2,1)S(1)}, ...), branch_computations={%region_5.5_spmd, %region_6.8_spmd} | conditional | flops 309985792 | bytes 21956620 | solution.py:46
  357.1 5.6 %fusion.66 = (f32[4,4,256]{2,1,0:T(4,128)}, f32[4,4,256,256]{2,3,1,0:T(8,128)}) fusion(f32[4,256,256]{1,2,0:T(8,128)} %convert_element_type.71, pred[256]{0:T(512)(128)(4,1)S(1)} %compare_reduce_fusion, bf16[4,256,4,32]{1,3,2,0:T(8,128)(2,1)} %bitcast.114, bf16[4,256,4,32]{1,3,2,0:T(8,128)(2,1)S(1)} %bitcast.113), kind=kOutput, calls=%fused_computation.88 | convolution fusion | flops 71303424 | bytes 5783808 | tf_op jit(solution)/shard_map/while/body/eval_jaxpr/cond/branch_1_fun/sub | solution.py:31
  362.9 2.7 fusion.5
  372.7 5.2 %gather_fusion = bf16[32,2,256,128]{3,2,1,0:T(8,128)(2,1)} fusion(bf16[32,2,256,128]{3,2,1,0:T(8,128)(2,1)} %bitcast.116, s32[1024]{0:T(1024)S(1)} %pad_clamp_fusion), kind=kCustom, calls=%fused_computation | custom fusion | bytes 8388736 | tf_op jit(solution)/shard_map/jit(_take)/gather | solution.py:93
  380.6 59.6 %all_to_all.5 = bf16[32,2,256,128]{3,2,1,0:T(8,128)(2,1)S(1)} all-to-all(bf16[32,2,256,128]{3,2,1,0:T(8,128)(2,1)S(1)} %broadcast_select_fusion), channel_id=1, replica_groups=mesh['sample'=32,'axial'=4] {'sample'}, dimensions={0} | all-to-all | bytes 8388608 | tf_op jit(solution)/shard_map/all_to_all | solution.py:94
  (369 shorter events, 218.4 us)
Async XLA Ops:
  0.0 10.8 %copy-start = (bf16[128,4]{0,1:T(4,128)(2,1)S(1)}, bf16[128,4]{0,1:T(4,128)(2,1)}, u32[]{:S(2)}) copy-start(bf16[128,4]{0,1:T(4,128)(2,1)} %param.16) | copy-start | bytes 3076
  0.0 3.5 copy-start.1
  0.0 10.2 %copy-start.4 = (s32[32]{0:T(128)S(1)}, s32[32]{0:T(128)}, u32[]{:S(2)}) copy-start(s32[32]{0:T(128)} %param.13) | copy-start | bytes 388
  32.0 8.8 %copy-start.2 = (bf16[128,512]{1,0:T(8,128)(2,1)S(1)}, bf16[128,512]{1,0:T(8,128)(2,1)}, u32[]{:S(2)}) copy-start(bf16[128,512]{1,0:T(8,128)(2,1)} %param.15) | copy-start | bytes 393220
  372.7 5.2 %copy-start.3 = (pred[32]{0:T(512)(128)(4,1)S(1)}, pred[32]{0:T(512)(128)(4,1)}, u32[]{:S(2)}) copy-start(pred[32]{0:T(512)(128)(4,1)} %compare_and_fusion) | copy-start | bytes 100
where the time goes:
time: 445 us; the launch traced here: 442 us
  matrix products  220 us (49%)
  other arithmetic  93 us (21%)
  blocking collectives  73 us (16%)
  local copies, waits for them, and re-layouts  44.3 us (10%)
  loops' own time  11.3 us (3%)
    sub x16, matrix products, attend(): weights = jax.nn.softmax(scores, axis=-1).astype(bf16)  88.8 us
    all_to_all x1, blocking collectives, shards(): lax.all_to_all(shuffled, 'sample', split_axis=0, concat_axis=0, tiled=True)  59.6 us
    dot_general x16, matrix products, attend(): jnp.einsum('grhjk,grkhd->grjhd', weights, values, preferred_element_type=...  42.7 us
    dot_general x16, matrix products, update_rows(): jnp.einsum('grlf,fc->grlc', hidden, w_down, preferred_element_type=f32)  39.1 us
    dot_general x16, matrix products, attend(): jnp.einsum('grlc,cf->grlf', normed, w_proj, preferred_element_type=f32)  21.9 us
    dot_general x16, matrix products, attend(): return jnp.einsum('grlf,fc->grlc', gated, w_out, preferred_element_type=f32)  21 us
    convert_element_type x16, other arithmetic, update_rows(): (block.astype(f32) + jnp.where(pair_live[..., None], update, 0.0)).astype...  18.6 us
    convert_element_type x16, other arithmetic, attend(): scores = jnp.einsum('grjhd,grkhd->grhjk', query, keys, preferred_element_...  18.5 us

commit v1 on v0

v1 whole, which is shorter than its diff:
```python
import functools

import jax
import jax.numpy as jnp
from jax import lax
from jax.experimental import pallas as pl
from jax.experimental.pallas import tpu as pltpu
from jax.sharding import PartitionSpec as P

F32 = jnp.float32
BF16 = jnp.bfloat16
LOG2E = 1.4426950408889634
DEAD = -1e9
NT = (((1,), (1,)), ((), ()))


def normalise(values_in):
    centre = values_in - jnp.mean(values_in, -1, keepdims=True)
    spread = jnp.mean(centre * centre, -1, keepdims=True)
    return centre * lax.rsqrt(spread + 1e-05)


def bias_kernel(x_ref, wb_ref, normed_ref, bias_ref, hold_ref):
    rows = x_ref.shape[0]
    heads = bias_ref.shape[0]
    for r in range(rows):
        normed = normalise(x_ref[r].astype(F32)).astype(BF16)
        normed_ref[r] = normed
        res = lax.dot_general(wb_ref[...], normed, NT, preferred_element_type=F32)
        for h in range(heads):
            hold_ref[h, r : r + 1, :] = res[h : h + 1]
    bias_ref[...] = hold_ref[...].astype(BF16)


def local_bias(local, w_bias):
    rows, width, chans = local.shape
    heads = w_bias.shape[1]
    step = 16
    wb = jnp.zeros((8, chans), BF16).at[:heads].set(w_bias.T)
    return pl.pallas_call(
        bias_kernel,
        name="bias",
        grid=(rows // step,),
        in_specs=[
            pl.BlockSpec((step, width, chans), lambda i: (i, 0, 0)),
            pl.BlockSpec((8, chans), lambda i: (0, 0)),
        ],
        out_specs=[
            pl.BlockSpec((step, width, chans), lambda i: (i, 0, 0)),
            pl.BlockSpec((heads, step, width), lambda i: (0, i, 0)),
        ],
        out_shape=[
            jax.ShapeDtypeStruct((rows, width, chans), BF16),
            jax.ShapeDtypeStruct((heads, rows, width), BF16),
        ],
        scratch_shapes=[pltpu.VMEM((heads, step, width), F32)],
        compiler_params=pltpu.CompilerParams(vmem_limit_bytes=48 * 1024 * 1024),
    )(local, wb)


def update_kernel(
    order_ref,
    info_ref,
    x_ref,
    n_ref,
    bias_ref,
    wp_ref,
    wo_ref,
    wu_ref,
    wd_ref,
    out_ref,
    bias_s,
    mid_s,
):
    step = pl.program_id(0)
    _, rows, width, chans = x_ref.shape
    heads = bias_ref.shape[0]
    inner = wp_ref.shape[1] // 4
    size_h = inner // heads
    length = info_ref[0]
    first = info_ref[1] + order_ref[step] * rows

    @pl.when(step == 0)
    def _():
        live = lax.broadcasted_iota(jnp.int32, (width, width), 1) < length
        for h in range(heads):
            bias_s[h] = jnp.where(live, bias_ref[h].astype(F32) * LOG2E, DEAD)

    lane = lax.broadcasted_iota(jnp.int32, (width, inner), 1)
    masks = [(lane >= h * size_h) & (lane < (h + 1) * size_h) for h in range(heads)]

    def attend(safe):
        bad = None
        for r in range(rows):
            normed = n_ref[0, r]
            proj = jnp.dot(normed, wp_ref[...], preferred_element_type=F32)
            query = (proj[:, :inner] * (size_h ** (-0.5) * LOG2E)).astype(BF16)
            keys = proj[:, inner : 2 * inner].astype(BF16)
            values = proj[:, 2 * inner : 3 * inner].astype(BF16)
            gate = jax.nn.sigmoid(proj[:, 3 * inner :])
            zero = jnp.zeros((), BF16)
            one = jnp.ones((), BF16)
            both = jnp.zeros((width, 2 * inner), F32)
            for h in range(heads):
                score = lax.dot_general(
                    jnp.where(masks[h], query, zero), keys, NT, preferred_element_type=F32
                )
                score = score + bias_s[h]
                if safe:
                    score = score - jnp.max(score, -1, keepdims=True)
                weight = jnp.exp2(score).astype(BF16)
                side = jnp.concatenate(
                    [jnp.where(masks[h], values, zero), jnp.where(masks[h], one, zero)], 1
                )
                both = both + jnp.dot(weight, side, preferred_element_type=F32)
            total = both[:, inner:]
            if not safe:
                low, high = jnp.min(total), jnp.max(total)
                good = (low > 1e-20) & (high < 1e30)
                bad = jnp.logical_not(good) if bad is None else bad | jnp.logical_not(good)
            gated = (gate * (both[:, :inner] / total)).astype(BF16)
            update = jnp.dot(gated, wo_ref[...], preferred_element_type=F32)
            place = lax.broadcasted_iota(jnp.int32, (width, chans), 0)
            live = (place < length) & (first + r < length)
            middle = x_ref[0, r].astype(F32) + jnp.where(live, update, 0.0)
            mid_s[r * width : (r + 1) * width] = middle.astype(BF16)
        return bad

    @pl.when(first < length)
    def _():
        bad = attend(False)

        @pl.when(bad)
        def _():
            attend(True)

    @pl.when(first >= length)
    def _():
        mid_s[...] = x_ref[0].reshape(rows * width, chans)

    middle = mid_s[...].astype(F32)
    normed_mid = normalise(middle).astype(BF16)
    hidden = jax.nn.relu(jnp.dot(normed_mid, wu_ref[...], preferred_element_type=F32)).astype(BF16)
    down = jnp.dot(hidden, wd_ref[...], preferred_element_type=F32)
    out_ref[...] = (middle + down).astype(BF16).reshape(out_ref.shape)


def update_blocks(order, info, blocks, normeds, bias, w_proj, w_out, w_up, w_down):
    count = order.shape[0]
    _, rows, width, chans = blocks.shape
    heads = bias.shape[0]
    whole = lambda *shape: pl.BlockSpec(shape, lambda i, o, n: (0,) * len(shape))
    picked = pl.BlockSpec((1, rows, width, chans), lambda i, o, n: (o[i], 0, 0, 0))
    return pl.pallas_call(
        update_kernel,
        name="update",
        grid_spec=pltpu.PrefetchScalarGridSpec(
            num_scalar_prefetch=2,
            grid=(count,),
            in_specs=[
                picked,
                picked,
                whole(heads, width, width),
                whole(*w_proj.shape),
                whole(*w_out.shape),
                whole(*w_up.shape),
                whole(*w_down.shape),
            ],
            out_specs=pl.BlockSpec((1, rows, width, chans), lambda i, o, n: (i, 0, 0, 0)),
            scratch_shapes=[
                pltpu.VMEM((heads, width, width), F32),
                pltpu.VMEM((rows * width, chans), BF16),
            ],
        ),
        out_shape=jax.ShapeDtypeStruct((count, rows, width, chans), BF16),
        compiler_params=pltpu.CompilerParams(vmem_limit_bytes=48 * 1024 * 1024),
    )(order, info, blocks, normeds, bias, w_proj, w_out, w_up, w_down)


def shards(pair, lengths, block_group, w_proj, w_bias, w_out, w_up, w_down):
    group_idx = lax.axis_index("sample")
    axial_idx = lax.axis_index("axial")
    groups_n = lax.axis_size("sample")
    _, ax_rows, width, chans = pair.shape
    blk_rows = ax_rows // groups_n
    local = pair[0]
    group_ids = jnp.arange(groups_n, dtype=jnp.int32)
    own_row = jnp.take(block_group, group_idx, axis=0)
    order = jnp.sum(jnp.where(own_row[None, :] == group_ids[:, None], group_ids[None, :], 0), 1)
    length = jnp.take(lengths, group_idx)
    info = jnp.stack([length, axial_idx * ax_rows]).astype(jnp.int32)
    normed, bias = local_bias(local, w_bias)
    crop_bias = lax.all_gather(bias, "axial", axis=1, tiled=True)
    shape = (groups_n, blk_rows, width, chans)
    updated = update_blocks(
        order, info, local.reshape(shape), normed.reshape(shape), crop_bias, w_proj, w_out, w_up, w_down
    )
    arrived = lax.all_to_all(updated, "sample", split_axis=0, concat_axis=0, tiled=True)
    return arrived.reshape(1, 1, groups_n, blk_rows, width, chans)


def solution(mesh):
    return jax.shard_map(
        shards,
        mesh=mesh,
        in_specs=(P("sample", "axial", None, None), P(), P(), P(), P(), P(), P(), P()),
        out_specs=P("sample", "axial", None, None, None, None),
        check_vma=False,
    )
```

time: 445 us -> 222 us (0.50)
  matrix products: 220 us -> 0 us
  Pallas kernels: 0 us -> 141 us
  other arithmetic: 93 us -> 0.88 us
  local copies, waits for them, and re-layouts: 44.3 us -> 6.02 us
  loops' own time: 11.3 us -> 0 us
    pallas_call x0 -> x2, Pallas kernels: none -> 141 us  [the longest x1 132 us: update_blocks(): pl.pallas_call(update_kernel, name='update', grid_spec=pltpu.PrefetchScal...]
    dot_general x65 -> x0, matrix products: 131 us -> none  [the longest x16 42.7 us: attend(): jnp.einsum('grhjk,grkhd->grjhd', weights, values, preferred_element_type=...]
    sub x16 -> x0, matrix products: 88.8 us -> none  [attend(): weights = jax.nn.softmax(scores, axis=-1).astype(bf16)]
    convert_element_type x49 -> x0, other arithmetic: 47 us -> none  [the longest x16 18.6 us: update_rows(): (block.astype(f32) + jnp.where(pair_live[..., None], update, 0.0)).astype...]
    reduce_sum x34 -> x0, other arithmetic: 16.8 us -> none  [the longest x17 10.9 us: layer_norm(): spread = jnp.mean(centre * centre, -1, keepdims=True)]
    reshape x16 -> x0, local copies, waits for them, and re-layouts: 16.1 us -> none  [attend(): attended = jnp.einsum('grhjk,grkhd->grjhd', weights, values, preferred_el...]
    convert_element_type x16 -> x0, local copies, waits for them, and re-layouts: 13.7 us -> none  [attend(): (projected[..., :inner] * size_h ** (-0.5)).astype(bf16).reshape(shape_h)]
    reduce_or x16 -> x0, other arithmetic: 11.4 us -> none  [update_rows(): jnp.any(pair_live)]
where the time goes in v1:
time: 222 us; the launch traced here: 221 us
  Pallas kernels  141 us (64%)
  blocking collectives  73 us (33%)
  local copies, waits for them, and re-layouts  6.02 us (3%)
    pallas_call x1, Pallas kernels, update_blocks(): pl.pallas_call(update_kernel, name='update', grid_spec=pltpu.PrefetchScal...  132 us
    all_to_all x1, blocking collectives, shards(): lax.all_to_all(updated, 'sample', split_axis=0, concat_axis=0, tiled=True)  59.6 us
    all_gather x1, blocking collectives, shards(): crop_bias = lax.all_gather(bias, 'axial', axis=1, tiled=True)  13.4 us
    pallas_call x1, Pallas kernels, local_bias(): pl.pallas_call(bias_kernel, name='bias', grid=(rows // step,), in_specs=[...  8.53 us

profile of v1, /device:TPU:1, one launch (start us, length us, event | category | flops | bytes accessed | tf_op | source)
XLA Modules:
  0.0 221.2 jit_solution(14023434426167748955)
XLA Ops:
  0.0 0.0 copy-start.3
  0.0 0.0 copy-start.2
  0.0 0.0 copy-start.4
  0.0 0.0 copy-start.1
  0.0 1.3 dynamic-slice.14
  1.3 0.7 fusion
  2.0 0.1 select_reduce_fusion.order_ref
  2.1 0.7 scatter.4.wb_ref
  2.8 8.5 %bias.1 = (bf16[64,256,128]{2,1,0:T(8,128)(2,1)S(1)}, bf16[4,64,256]{2,1,0:T(8,128)(2,1)S(1)}) custom-call(bf16[64,256,128]{2,1,0:T(8,128)(2,1)} %bitcast.11, bf16[8,128]{1,0:T(8,128)(2,1)S(1)} %scatter.4.wb_ref), custom_call_target="tpu_custom_call" | custom-call | tf_op jit(solution)/shard_map/bias/pallas_call | solution.py:40
  11.4 0.0 copy-start
  11.4 2.0 copy-done
  13.4 13.4 %all_gather.3.bias_ref = bf16[4,256,256]{2,1,0:T(8,128)(2,1)S(1)} all-gather(bf16[4,64,256]{2,1,0:T(8,128)(2,1)S(1)} %get-tuple-element.20), channel_id=1, replica_groups=mesh['sample'=32,'axial'=4] {'axial'}, dimensions={1}, use_global_device_ids=true | all-gather | bytes 655360 | tf_op jit(solution)/shard_map/all_gather | solution.py:193
  27.4 0.1 pad_add_fusion.info_ref
  27.4 0.0 copy-done.3
  27.5 0.0 copy-done.2
  27.5 0.0 copy-done.4
  27.5 0.0 copy-done.1
  27.5 132.1 %update.1 = bf16[32,2,256,128]{3,2,1,0:T(8,128)(2,1)S(1)} custom-call(s32[32]{0:T(128)S(1)} %select_reduce_fusion.order_ref, s32[2]{0:T(128)S(1)} %pad_add_fusion.info_ref, bf16[32,2,256,128]{3,2,1,0:T(8,128)(2,1)} %bitcast.12, bf16[32,2,256,128]{3,2,1,0:T(8,128)(2,1)} %bitcast.10, bf16[4,256,256]{2,1,0:T(8,128)(2,1)S(1)} %all_gather.3.bias_ref, ...), custom_call_target="tpu_custom_call" | custom-call | tf_op jit(solution)/shard_map/update/pallas_call | solution.py:154
  159.6 59.6 %all_to_all.5 = bf16[32,2,256,128]{3,2,1,0:T(8,128)(2,1)S(1)} all-to-all(bf16[32,2,256,128]{3,2,1,0:T(8,128)(2,1)S(1)} %update.1), channel_id=1, replica_groups=mesh['sample'=32,'axial'=4] {'sample'}, dimensions={0} | all-to-all | bytes 8388608 | tf_op jit(solution)/shard_map/all_to_all | solution.py:198
  219.2 2.0 copy.10
Async XLA Ops:
  0.0 27.5 %copy-start.3 = (bf16[512,128]{1,0:T(8,128)(2,1)S(1)}, bf16[512,128]{1,0:T(8,128)(2,1)}, u32[]{:S(2)}) copy-start(bf16[512,128]{1,0:T(8,128)(2,1)} %wd_ref.1) | copy-start | bytes 393220
  0.0 27.5 %copy-start.2 = (bf16[128,512]{1,0:T(8,128)(2,1)S(1)}, bf16[128,512]{1,0:T(8,128)(2,1)}, u32[]{:S(2)}) copy-start(bf16[128,512]{1,0:T(8,128)(2,1)} %wu_ref.1) | copy-start | bytes 393220
  0.0 27.5 %copy-start.4 = (bf16[128,128]{1,0:T(8,128)(2,1)S(1)}, bf16[128,128]{1,0:T(8,128)(2,1)}, u32[]{:S(2)}) copy-start(bf16[128,128]{1,0:T(8,128)(2,1)} %wo_ref.1) | copy-start | bytes 98308
  0.0 27.4 %copy-start.1 = (bf16[128,512]{1,0:T(8,128)(2,1)S(1)}, bf16[128,512]{1,0:T(8,128)(2,1)}, u32[]{:S(2)}) copy-start(bf16[128,512]{1,0:T(8,128)(2,1)} %wp_ref.1) | copy-start | bytes 393220
  11.4 2.0 copy-start

commit v2 on v0

v2 whole, which is shorter than its diff:
```python
import functools

import jax
import jax.numpy as jnp
from jax import lax
from jax.experimental import pallas as pl
from jax.experimental.pallas import tpu as pltpu
from jax.sharding import PartitionSpec as P

F32 = jnp.float32
BF16 = jnp.bfloat16
LOG2E = 1.4426950408889634
DEAD = -1e9
NT = (((1,), (1,)), ((), ()))


def normalise(values_in):
    centre = values_in - jnp.mean(values_in, -1, keepdims=True)
    spread = jnp.mean(centre * centre, -1, keepdims=True)
    return centre * lax.rsqrt(spread + 1e-05)


def bias_kernel(x_hbm, wb_ref, x_ref, normed_ref, bias_ref, hold_ref, sems):
    rows = x_ref.shape[0]
    heads = bias_ref.shape[0]
    parts = sems.shape[0]
    span = rows // parts
    copies = []
    for p in range(parts):
        part = pl.ds(p * span, span)
        copies.append(pltpu.make_async_copy(x_hbm.at[part], x_ref.at[part], sems.at[p]))
        copies[-1].start()
    for p in range(parts):
        copies[p].wait()
        for r in range(p * span, (p + 1) * span):
            normed = normalise(x_ref[r].astype(F32)).astype(BF16)
            normed_ref[r] = normed
            res = lax.dot_general(wb_ref[...], normed, NT, preferred_element_type=F32)
            for h in range(heads):
                hold_ref[h, r : r + 1, :] = res[h : h + 1]
    bias_ref[...] = hold_ref[...].astype(BF16)


def local_bias(local, w_bias):
    rows, width, chans = local.shape
    heads = w_bias.shape[1]
    wb = jnp.zeros((8, chans), BF16).at[:heads].set(w_bias.T)
    vmem = pl.BlockSpec(memory_space=pltpu.VMEM)
    return pl.pallas_call(
        bias_kernel,
        name="bias",
        in_specs=[pl.BlockSpec(memory_space=pl.ANY), vmem],
        out_specs=[vmem, vmem, vmem],
        out_shape=[
            jax.ShapeDtypeStruct((rows, width, chans), BF16),
            jax.ShapeDtypeStruct((rows, width, chans), BF16),
            jax.ShapeDtypeStruct((heads, rows, width), BF16),
        ],
        scratch_shapes=[pltpu.VMEM((heads, rows, width), F32), pltpu.SemaphoreType.DMA((8,))],
        compiler_params=pltpu.CompilerParams(vmem_limit_bytes=32 * 1024 * 1024),
    )(local, wb)


def masked_bias(bias, length):
    live = jnp.arange(bias.shape[-1], dtype=jnp.int32) < length
    return jnp.where(live, bias.astype(F32) * LOG2E, DEAD)


def update_kernel(
    order_ref, info_ref, x_ref, n_ref, bias_ref, wp_ref, wo_ref, wu_ref, wd_ref, out_ref, sum_s, low_s, high_s
):
    _, rows, width, chans = x_ref.shape
    heads = bias_ref.shape[0]
    inner = wp_ref.shape[1] // 4
    size_h = inner // heads
    length = info_ref[0]
    lane = lax.broadcasted_iota(jnp.int32, (width, inner), 1)
    zero = jnp.zeros((), BF16)

    def head_mask(h):
        return (lane >= h * size_h) & (lane < (h + 1) * size_h)

    masks = [head_mask(h) for h in range(heads)]

    def project(block, r):
        proj = jnp.dot(n_ref[block, r], wp_ref[...], preferred_element_type=F32)
        query = (proj[:, :inner] * (size_h ** (-0.5) * LOG2E)).astype(BF16)
        keys = proj[:, inner : 2 * inner].astype(BF16)
        values = proj[:, 2 * inner : 3 * inner].astype(BF16)
        return query, keys, jnp.concatenate([values, jnp.ones_like(values)], 1), proj[:, 3 * inner :]

    def score_of(query, keys, mask, h):
        score = lax.dot_general(jnp.where(mask, query, zero), keys, NT, preferred_element_type=F32)
        return score + bias_ref[h]

    def weigh(score, side):
        return jnp.dot(jnp.exp2(score).astype(BF16), side, preferred_element_type=F32)

    def close(block, first, r, both, gate):
        gated = (jax.nn.sigmoid(gate) * (both[:, :inner] / both[:, inner:])).astype(BF16)
        update = jnp.dot(gated, wo_ref[...], preferred_element_type=F32)
        place = lax.broadcasted_iota(jnp.int32, (width, chans), 0)
        live = (place < length) & (first + r < length)
        middle = x_ref[block, r].astype(F32) + jnp.where(live, update, 0.0)
        return middle.astype(BF16)

    def finish(middle):
        middle = middle.astype(F32)
        normed_mid = normalise(middle).astype(BF16)
        hidden = jnp.dot(normed_mid, wu_ref[...], preferred_element_type=F32)
        hidden = jax.nn.relu(hidden).astype(BF16)
        down = jnp.dot(hidden, wd_ref[...], preferred_element_type=F32)
        return (middle + down).astype(BF16)

    def attend(i, block, first):
        ends = []
        mids = []
        for r in range(rows):
            query, keys, side, gate = project(block, r)
            both = None
            for h in range(heads):
                each = weigh(score_of(query, keys, masks[h], h), side)
                mask = jnp.concatenate([masks[h], masks[h]], 1)
                both = each if both is None else jnp.where(mask, each, both)
            mids.append(close(block, first, r, both, gate))
            ends.append(both[:, inner:])
        out_ref[i] = finish(jnp.concatenate(mids, 0)).reshape(rows, width, chans)
        low = functools.reduce(jnp.minimum, ends)
        high = functools.reduce(jnp.maximum, ends)
        low_s[...] = jnp.minimum(low_s[...], jnp.min(low.reshape(-1, 8, inner), 0))
        high_s[...] = jnp.maximum(high_s[...], jnp.max(high.reshape(-1, 8, inner), 0))

    def attend_safe(i, block, first):
        def one_row(r, carry):
            query, keys, side, gate = project(block, r)

            def one_head(h, carry):
                mask = head_mask(h)
                score = score_of(query, keys, mask, h)
                each = weigh(score - jnp.max(score, -1, keepdims=True), side)
                sum_s[...] = jnp.where(jnp.concatenate([mask, mask], 1), each, sum_s[...])
                return carry

            lax.fori_loop(0, heads, one_head, 0)
            out_ref[i, r] = finish(close(block, first, r, sum_s[...], gate))
            return carry

        lax.fori_loop(0, rows, one_row, 0)

    count = out_ref.shape[0]
    low_s[...] = jnp.ones_like(low_s)
    high_s[...] = jnp.ones_like(high_s)

    def one_block(i, carry):
        block = order_ref[i]
        first = info_ref[1] + block * rows

        @pl.when(first < length)
        def _():
            attend(i, block, first)

        @pl.when(first >= length)
        def _():
            out_ref[i] = finish(x_ref[block].reshape(rows * width, chans)).reshape(rows, width, chans)

        return carry

    lax.fori_loop(0, count, one_block, 0, unroll=1)
    good = (jnp.min(low_s[...]) > 1e-20) & (jnp.max(high_s[...]) < 1e30)

    @pl.when(jnp.logical_not(good))
    def _():
        def again(i, carry):
            block = order_ref[i]
            first = info_ref[1] + block * rows

            @pl.when(first < length)
            def _():
                attend_safe(i, block, first)

            return carry

        lax.fori_loop(0, count, again, 0)


def update_blocks(order, info, blocks, normeds, bias, w_proj, w_out, w_up, w_down):
    count = order.shape[0]
    _, rows, width, chans = blocks.shape
    vmem = pl.BlockSpec(memory_space=pltpu.VMEM)
    smem = pl.BlockSpec(memory_space=pltpu.SMEM)
    work = 2 * rows * width * chans * count * (12 * chans + 4 * width)
    return pl.pallas_call(
        update_kernel,
        name="update",
        in_specs=[smem, smem] + [vmem] * 7,
        out_specs=vmem,
        out_shape=jax.ShapeDtypeStruct((count, rows, width, chans), BF16),
        scratch_shapes=[
            pltpu.VMEM((width, w_proj.shape[1] // 2), F32),
            pltpu.VMEM((8, w_proj.shape[1] // 4), F32),
            pltpu.VMEM((8, w_proj.shape[1] // 4), F32),
        ],
        cost_estimate=pl.CostEstimate(flops=8 * work, bytes_accessed=0, transcendentals=0),
        compiler_params=pltpu.CompilerParams(vmem_limit_bytes=16 * 1024 * 1024),
    )(order, info, blocks, normeds, bias, w_proj, w_out, w_up, w_down)


def place_kernel(where_ref, *refs):
    count = where_ref.shape[0]
    parts, out_ref, sems = refs[:count], refs[count], refs[count + 1]
    copies = [
        pltpu.make_async_copy(parts[t], out_ref.at[pl.ds(where_ref[t], 1)], sems.at[t])
        for t in range(count)
    ]
    for copy in copies:
        copy.start()
    for copy in copies:
        copy.wait()


def place_parts(where, parts):
    anywhere = pl.BlockSpec(memory_space=pl.ANY)
    count = len(parts)
    return pl.pallas_call(
        place_kernel,
        name="place",
        in_specs=[pl.BlockSpec(memory_space=pltpu.SMEM)] + [anywhere] * count,
        out_specs=anywhere,
        out_shape=jax.ShapeDtypeStruct((count,) + parts[0].shape[1:], BF16),
        scratch_shapes=[pltpu.SemaphoreType.DMA((count,))],
    )(where, *parts)


def shift_order():
    pairs = [(1, 1), (3, 3), (1, 3), (3, 1), (2, 0), (0, 2), (1, 0), (3, 0), (0, 1), (0, 3)]
    pairs += [(2, 1), (2, 3), (1, 2), (3, 2), (2, 2), (0, 0)]
    return [(dx, dy, dc) for dx, dy in pairs for dc in (1, 0)]


def moved(group, shift, sign):
    dx, dy, dc = shift
    x, y, c = group // 8, (group // 2) % 4, group % 2
    return (((x + sign * dx) % 4) * 4 + (y + sign * dy) % 4) * 2 + (c + dc) % 2


def shards(pair, lengths, block_group, w_proj, w_bias, w_out, w_up, w_down):
    group_idx = lax.axis_index("sample")
    axial_idx = lax.axis_index("axial")
    groups_n = lax.axis_size("sample")
    _, ax_rows, width, chans = pair.shape
    blk_rows = ax_rows // groups_n
    local = pair[0]
    group_ids = jnp.arange(groups_n, dtype=jnp.int32)
    own_row = jnp.take(block_group, group_idx, axis=0)
    shifts = shift_order()
    steps = jnp.asarray(shifts, jnp.int32)
    targets = moved(group_idx, steps.T, 1)
    sources = moved(group_idx, steps.T, -1).astype(jnp.int32)
    order = jnp.sum(jnp.where(own_row[None, :] == targets[:, None], group_ids[None, :], 0), 1)
    length = jnp.take(lengths, group_idx)
    info = jnp.stack([length, axial_idx * ax_rows]).astype(jnp.int32)
    local, normed, bias = local_bias(local, w_bias)
    crop_bias = masked_bias(lax.all_gather(bias, "axial", axis=1, tiled=True), length)
    shape = (groups_n, blk_rows, width, chans)
    local, normed = local.reshape(shape), normed.reshape(shape)
    parts = []
    span = 4
    for start in range(0, groups_n, span):
        updated = update_blocks(
            order[start : start + span],
            info,
            local,
            normed,
            crop_bias,
            w_proj,
            w_out,
            w_up,
            w_down,
        )
        if start >= span:
            before = parts[start - span : start]
            info, updated, before = lax.optimization_barrier((info, updated, before))
            parts[start - span : start] = before
        else:
            info, updated = lax.optimization_barrier((info, updated))
        for t in range(start, start + span):
            part = updated[t - start : t - start + 1]
            if any(shifts[t]):
                pairs = [(g, moved(g, shifts[t], 1)) for g in range(groups_n)]
                part = lax.ppermute(part, "sample", pairs)
            parts.append(part)
    out = place_parts(sources, parts)
    return out.reshape(1, 1, groups_n, blk_rows, width, chans)


def solution(mesh):
    return jax.shard_map(
        shards,
        mesh=mesh,
        in_specs=(P("sample", "axial", None, None), P(), P(), P(), P(), P(), P(), P()),
        out_specs=P("sample", "axial", None, None, None, None),
        check_vma=False,
    )
```

time: 445 us -> 475 us (1.067)
  Pallas kernels: 0 us -> 369 us
  matrix products: 220 us -> 0 us
  other arithmetic: 93 us -> 2.34 us
  blocking collectives: 73 us -> 13.4 us
  starting transfers between devices: 0 us -> 57.7 us
  local copies, waits for them, and re-layouts: 44.3 us -> 14.4 us
  loops' own time: 11.3 us -> 0 us
  waiting for transfers between devices: 0 us -> 8.52 us
    pallas_call x0 -> x10, Pallas kernels: none -> 369 us  [the longest x8 233 us: update_blocks(): pl.pallas_call(update_kernel, name='update', in_specs=[smem, smem] + [vme...]
    dot_general x65 -> x0, matrix products: 131 us -> none  [the longest x16 42.7 us: attend(): jnp.einsum('grhjk,grkhd->grjhd', weights, values, preferred_element_type=...]
    sub x16 -> x0, matrix products: 88.8 us -> none  [attend(): weights = jax.nn.softmax(scores, axis=-1).astype(bf16)]
    all_to_all x1 -> x0, blocking collectives: 59.6 us -> none  [shards(): lax.all_to_all(shuffled, 'sample', split_axis=0, concat_axis=0, tiled=True)]
    ppermute x0 -> x31, starting transfers between devices: none -> 57.7 us  [shards(): part = lax.ppermute(part, 'sample', pairs)]
    convert_element_type x49 -> x0, other arithmetic: 47 us -> none  [the longest x16 18.6 us: update_rows(): (block.astype(f32) + jnp.where(pair_live[..., None], update, 0.0)).astype...]
    reduce_sum x35 -> x1, other arithmetic: 16.9 us -> 0.18 us  [shards(): jnp.sum(jnp.where(own_row[None, :] == targets[:, None], group_ids[None, :...]
    reshape x16 -> x0, local copies, waits for them, and re-layouts: 16.1 us -> none  [attend(): attended = jnp.einsum('grhjk,grkhd->grjhd', weights, values, preferred_el...]
  transfers between devices with their start and end apart: 0 -> 31, of which waited for: 0 -> 2; matrix products, arithmetic and copies ran while one was open for 0% -> 0% of each run, Pallas kernels for 0% -> 44%
where the time goes in v2:
time: 475 us; the launch traced here: 468 us
  Pallas kernels  369 us (78%)
  starting transfers between devices  57.7 us (12%)
  local copies, waits for them, and re-layouts  14.4 us (3%)
  blocking collectives  13.4 us (3%)
  waiting for transfers between devices  8.52 us (2%)
    pallas_call x8, Pallas kernels, update_blocks(): pl.pallas_call(update_kernel, name='update', in_specs=[smem, smem] + [vme...  233 us
    pallas_call x1, Pallas kernels, place_parts(): pl.pallas_call(place_kernel, name='place', in_specs=[pl.BlockSpec(memory_...  129 us
    ppermute x31, starting transfers between devices, shards(): part = lax.ppermute(part, 'sample', pairs)  57.7 us
    all_gather x1, blocking collectives, shards(): lax.all_gather(bias, 'axial', axis=1, tiled=True)  13.4 us
    unnamed x84, local copies, waits for them, and re-layouts  11.3 us
  transfers between devices with their start and end apart: 31, of which 2 were waited for; matrix products, arithmetic and copies ran while one was open for 0% of the time, Pallas kernels for 44%

profile of v2, /device:TPU:1, one launch (start us, length us, event | category | flops | bytes accessed | tf_op | source)
XLA Modules:
  0.0 467.7 jit_solution(2446653069036753024)
XLA Ops:
  0.0 1.3 dynamic-slice.13
  1.3 0.7 fusion.2
  2.7 0.7 multiply_add_fusion
  3.6 0.7 scatter.4.wb_ref
  4.3 2.2 copy-done
  6.5 7.7 %bias.1 = (bf16[64,256,128]{2,1,0:T(8,128)(2,1)S(1)}, bf16[64,256,128]{2,1,0:T(8,128)(2,1)S(1)}, bf16[4,64,256]{2,1,0:T(8,128)(2,1)S(1)}) custom-call(bf16[64,256,128]{2,1,0:T(8,128)(2,1)S(1)} %bitcast.29, bf16[8,128]{1,0:T(8,128)(2,1)S(1)} %scatter.4.wb_ref), custom_call_target="tpu_custom_call" | custom-call | tf_op jit(solution)/shard_map/bias/pallas_call | solution.py:49
  14.2 2.0 copy-done.1
  16.2 2.0 copy-done.3
  18.2 13.4 %all_gather.3 = bf16[4,256,256]{2,1,0:T(8,128)(2,1)S(1)} all-gather(bf16[4,64,256]{2,1,0:T(8,128)(2,1)S(1)} %get-tuple-element.65), channel_id=1, replica_groups=mesh['sample'=32,'axial'=4] {'axial'}, dimensions={1}, use_global_device_ids=true | all-gather | bytes 655360 | tf_op jit(solution)/shard_map/all_gather | solution.py:263
  31.8 2.2 copy-done.2
  34.0 2.2 copy-done.4
  36.2 29.0 %update.8 = bf16[4,2,256,128]{3,2,1,0:T(8,128)(2,1)S(1)} custom-call(s32[4]{0:T(128)S(1)} %get-tuple-element.172.order_ref, s32[2]{0:T(128)S(1)} %pad_add_fusion.info_ref, bf16[32,2,256,128]{3,2,1,0:T(8,128)(2,1)S(1)} %bitcast.30, bf16[32,2,256,128]{3,2,1,0:T(8,128)(2,1)S(1)} %bitcast.38, f32[4,256,256]{2,1,0:T(8,128)S(1)} %multiply_select_fusion.bias_ref, ...), custom_call_target="tpu_custom_call" | custom-call | flops 10737418240 | tf_op jit(solution)/shard_map/update/pallas_call | solution.py:192
  65.3 5.0 %collective-permute-start.3 = (bf16[1,2,256,128]{3,2,1,0:T(8,128)(2,1)S(1)}, bf16[1,2,256,128]{3,2,1,0:T(8,128)(2,1)S(1)}, u32[]{:S(2)}, u32[]{:S(2)}) collective-permute-start(bf16[1,2,256,128]{3,2,1,0:T(8,128)(2,1)S(1)} %get-tuple-element.161), channel_id=1, source_target_pairs={{0,120},{4,124},{8,96},{12,100},{16,104},{20,108},{24,112},{28,116... | collective-permute-start | bytes 393224 | tf_op jit(solution)/shard_map/ppermute | solution.py:290
  70.3 3.0 collective-permute-start.2
  73.3 1.6 collective-permute-start.1
  75.1 29.0 %update.9 = bf16[4,2,256,128]{3,2,1,0:T(8,128)(2,1)S(1)} custom-call(s32[4]{0:T(128)S(1)} %get-tuple-element.171.order_ref, s32[2]{0:T(128)S(1)} %pad_add_fusion.info_ref, bf16[32,2,256,128]{3,2,1,0:T(8,128)(2,1)S(1)} %bitcast.31, bf16[32,2,256,128]{3,2,1,0:T(8,128)(2,1)S(1)} %bitcast.39, f32[4,256,256]{2,1,0:T(8,128)S(1)} %multiply_select_fusion.bias_ref, ...), custom_call_target="tpu_custom_call" | custom-call | flops 10737418240 | tf_op jit(solution)/shard_map/update/pallas_call | solution.py:192
  104.3 0.5 collective-permute-start.7
  104.7 5.0 %collective-permute-start.6 = (bf16[1,2,256,128]{3,2,1,0:T(8,128)(2,1)S(1)}, bf16[1,2,256,128]{3,2,1,0:T(8,128)(2,1)S(1)}, u32[]{:S(2)}, u32[]{:S(2)}) collective-permute-start(bf16[1,2,256,128]{3,2,1,0:T(8,128)(2,1)S(1)} %get-tuple-element.158), channel_id=1, source_target_pairs={{0,108},{4,104},{8,116},{12,112},{16,124},{20,120},{24,100},{28,96... | collective-permute-start | bytes 393224 | tf_op jit(solution)/shard_map/ppermute | solution.py:290
  109.8 0.8 collective-permute-start.5
  110.9 29.0 %update.10 = bf16[4,2,256,128]{3,2,1,0:T(8,128)(2,1)S(1)} custom-call(s32[4]{0:T(128)S(1)} %get-tuple-element.170.order_ref, s32[2]{0:T(128)S(1)} %pad_add_fusion.info_ref, bf16[32,2,256,128]{3,2,1,0:T(8,128)(2,1)S(1)} %bitcast.32, bf16[32,2,256,128]{3,2,1,0:T(8,128)(2,1)S(1)} %bitcast.40, f32[4,256,256]{2,1,0:T(8,128)S(1)} %multiply_select_fusion.bias_ref, ...), custom_call_target="tpu_custom_call" | custom-call | flops 10737418240 | tf_op jit(solution)/shard_map/update/pallas_call | solution.py:192
  140.1 2.4 collective-permute-start.11
  142.5 1.1 collective-permute-start.10
  143.6 3.4 collective-permute-start.9
  147.3 29.0 %update.11 = bf16[4,2,256,128]{3,2,1,0:T(8,128)(2,1)S(1)} custom-call(s32[4]{0:T(128)S(1)} %get-tuple-element.169.order_ref, s32[2]{0:T(128)S(1)} %pad_add_fusion.info_ref, bf16[32,2,256,128]{3,2,1,0:T(8,128)(2,1)S(1)} %bitcast.33, bf16[32,2,256,128]{3,2,1,0:T(8,128)(2,1)S(1)} %bitcast.41, f32[4,256,256]{2,1,0:T(8,128)S(1)} %multiply_select_fusion.bias_ref, ...), custom_call_target="tpu_custom_call" | custom-call | flops 10737418240 | tf_op jit(solution)/shard_map/update/pallas_call | solution.py:192
  176.5 2.4 collective-permute-start.15
  178.9 1.2 collective-permute-start.14
  180.1 0.9 collective-permute-start.13
  181.1 29.0 %update.12 = bf16[4,2,256,128]{3,2,1,0:T(8,128)(2,1)S(1)} custom-call(s32[4]{0:T(128)S(1)} %get-tuple-element.168.order_ref, s32[2]{0:T(128)S(1)} %pad_add_fusion.info_ref, bf16[32,2,256,128]{3,2,1,0:T(8,128)(2,1)S(1)} %bitcast.34, bf16[32,2,256,128]{3,2,1,0:T(8,128)(2,1)S(1)} %bitcast.42, f32[4,256,256]{2,1,0:T(8,128)S(1)} %multiply_select_fusion.bias_ref, ...), custom_call_target="tpu_custom_call" | custom-call | flops 10737418240 | tf_op jit(solution)/shard_map/update/pallas_call | solution.py:192
  210.3 2.2 collective-permute-start.19
  212.5 1.1 collective-permute-start.18
  213.6 1.0 collective-permute-start.17
  214.6 29.0 %update.13 = bf16[4,2,256,128]{3,2,1,0:T(8,128)(2,1)S(1)} custom-call(s32[4]{0:T(128)S(1)} %get-tuple-element.167.order_ref, s32[2]{0:T(128)S(1)} %pad_add_fusion.info_ref, bf16[32,2,256,128]{3,2,1,0:T(8,128)(2,1)S(1)} %bitcast.35, bf16[32,2,256,128]{3,2,1,0:T(8,128)(2,1)S(1)} %bitcast.43, f32[4,256,256]{2,1,0:T(8,128)S(1)} %multiply_select_fusion.bias_ref, ...), custom_call_target="tpu_custom_call" | custom-call | flops 10737418240 | tf_op jit(solution)/shard_map/update/pallas_call | solution.py:192
  243.8 5.1 %collective-permute-start.23 = (bf16[1,2,256,128]{3,2,1,0:T(8,128)(2,1)S(1)}, bf16[1,2,256,128]{3,2,1,0:T(8,128)(2,1)S(1)}, u32[]{:S(2)}, u32[]{:S(2)}) collective-permute-start(bf16[1,2,256,128]{3,2,1,0:T(8,128)(2,1)S(1)} %get-tuple-element.141), channel_id=1, source_target_pairs={{0,88},{4,92},{8,64},{12,68},{16,72},{20,76},{24,80},{28,84},{32,1... | collective-permute-start | bytes 393224 | tf_op jit(solution)/shard_map/ppermute | solution.py:290
  248.8 1.1 collective-permute-start.22
  249.9 3.6 collective-permute-start.21
  253.5 29.3 %update.14 = bf16[4,2,256,128]{3,2,1,0:T(8,128)(2,1)S(1)} custom-call(s32[4]{0:T(128)S(1)} %get-tuple-element.166.order_ref, s32[2]{0:T(128)S(1)} %pad_add_fusion.info_ref, bf16[32,2,256,128]{3,2,1,0:T(8,128)(2,1)S(1)} %bitcast.36, bf16[32,2,256,128]{3,2,1,0:T(8,128)(2,1)S(1)} %bitcast.44, f32[4,256,256]{2,1,0:T(8,128)S(1)} %multiply_select_fusion.bias_ref, ...), custom_call_target="tpu_custom_call" | custom-call | flops 10737418240 | tf_op jit(solution)/shard_map/update/pallas_call | solution.py:192
  283.0 4.9 %collective-permute-start.27 = (bf16[1,2,256,128]{3,2,1,0:T(8,128)(2,1)S(1)}, bf16[1,2,256,128]{3,2,1,0:T(8,128)(2,1)S(1)}, u32[]{:S(2)}, u32[]{:S(2)}) collective-permute-start(bf16[1,2,256,128]{3,2,1,0:T(8,128)(2,1)S(1)} %get-tuple-element.137), channel_id=1, source_target_pairs={{0,112},{4,116},{8,120},{12,124},{16,96},{20,100},{24,104},{28,108... | collective-permute-start | bytes 393224 | tf_op jit(solution)/shard_map/ppermute | solution.py:290
  287.9 0.5 collective-permute-start.26
  288.4 4.1 collective-permute-start.25
  292.5 29.0 %update.15 = bf16[4,2,256,128]{3,2,1,0:T(8,128)(2,1)S(1)} custom-call(s32[4]{0:T(128)S(1)} %get-tuple-element.165.order_ref, s32[2]{0:T(128)S(1)} %pad_add_fusion.info_ref, bf16[32,2,256,128]{3,2,1,0:T(8,128)(2,1)S(1)} %bitcast.37, bf16[32,2,256,128]{3,2,1,0:T(8,128)(2,1)S(1)} %bitcast.45, f32[4,256,256]{2,1,0:T(8,128)S(1)} %multiply_select_fusion.bias_ref, ...), custom_call_target="tpu_custom_call" | custom-call | flops 10737418240 | tf_op jit(solution)/shard_map/update/pallas_call | solution.py:192
  321.7 0.8 fusion.10
  322.4 0.4 collective-permute-start.30
  322.9 5.3 %collective-permute-start.29 = (bf16[1,2,256,128]{3,2,1,0:T(8,128)(2,1)S(1)}, bf16[1,2,256,128]{3,2,1,0:T(8,128)(2,1)S(1)}, u32[]{:S(2)}, u32[]{:S(2)}) collective-permute-start(bf16[1,2,256,128]{3,2,1,0:T(8,128)(2,1)S(1)} %get-tuple-element.135), channel_id=1, source_target_pairs={{0,80},{4,84},{8,88},{12,92},{16,64},{20,68},{24,72},{28,76},{32,1... | collective-permute-start | bytes 393224 | tf_op jit(solution)/shard_map/ppermute | solution.py:290
  328.5 0.5 multiply_add_fusion.1.where_ref
  329.0 2.8 collective-permute-done.29.refs_29_
  331.9 5.6 %collective-permute-done.28.refs_28_ = bf16[1,2,256,128]{3,2,1,0:T(8,128)(2,1)S(1)} collective-permute-done((bf16[1,2,256,128]{3,2,1,0:T(8,128)(2,1)S(1)}, bf16[1,2,256,128]{3,2,1,0:T(8,128)(2,1)S(1)}, u32[]{:S(2)}, u32[]{:S(2)}) %collective-permute-start.28) | collective-permute-done | bytes 131104 | tf_op jit(solution)/shard_map/ppermute | solution.py:290
  337.5 0.6 copy-done.39
  338.1 129.1 %place.1 = bf16[32,2,256,128]{3,2,1,0:T(8,128)(2,1)} custom-call(s32[32]{0:T(128)} %multiply_add_fusion.1.where_ref, bf16[1,2,256,128]{3,2,1,0:T(8,128)(2,1)} %copy-done.12, bf16[1,2,256,128]{3,2,1,0:T(8,128)(2,1)} %copy-done.11, bf16[1,2,256,128]{3,2,1,0:T(8,128)(2,1)} %copy-done.10, bf16[1,2,256,128]{3,2,1,0:T(8,128)(2,1)} %copy-done.9, ...), custom_call_target="tpu_custom_call" | custom-call | tf_op jit(solution)/shard_map/place/pallas_call | solution.py:224
  (127 shorter events, 1.9 us)
Async XLA Ops:
  65.3 38.8 %collective-permute-start.3 = (bf16[1,2,256,128]{3,2,1,0:T(8,128)(2,1)S(1)}, bf16[1,2,256,128]{3,2,1,0:T(8,128)(2,1)S(1)}, u32[]{:S(2)}, u32[]{:S(2)}) collective-permute-start(bf16[1,2,256,128]{3,2,1,0:T(8,128)(2,1)S(1)} %get-tuple-element.161), channel_id=1, source_target_pairs={{0,120},{4,124},{8,96},{12,100},{16,104},{20,108},{24,112},{28,116... | collective-permute-start | bytes 393224 | tf_op jit(solution)/shard_map/ppermute | solution.py:290
  70.3 33.9 %collective-permute-start.2 = (bf16[1,2,256,128]{3,2,1,0:T(8,128)(2,1)S(1)}, bf16[1,2,256,128]{3,2,1,0:T(8,128)(2,1)S(1)}, u32[]{:S(2)}, u32[]{:S(2)}) collective-permute-start(bf16[1,2,256,128]{3,2,1,0:T(8,128)(2,1)S(1)} %get-tuple-element.162), channel_id=1, source_target_pairs={{0,124},{4,120},{8,100},{12,96},{16,108},{20,104},{24,116},{28,112... | collective-permute-start | bytes 393224 | tf_op jit(solution)/shard_map/ppermute | solution.py:290
  73.3 30.9 %collective-permute-start.1 = (bf16[1,2,256,128]{3,2,1,0:T(8,128)(2,1)S(1)}, bf16[1,2,256,128]{3,2,1,0:T(8,128)(2,1)S(1)}, u32[]{:S(2)}, u32[]{:S(2)}) collective-permute-start(bf16[1,2,256,128]{3,2,1,0:T(8,128)(2,1)S(1)} %get-tuple-element.163), channel_id=1, source_target_pairs={{0,40},{4,44},{8,48},{12,52},{16,56},{20,60},{24,32},{28,36},{32,7... | collective-permute-start | bytes 393224 | tf_op jit(solution)/shard_map/ppermute | solution.py:290
  74.9 29.3 %collective-permute-start = (bf16[1,2,256,128]{3,2,1,0:T(8,128)(2,1)S(1)}, bf16[1,2,256,128]{3,2,1,0:T(8,128)(2,1)S(1)}, u32[]{:S(2)}, u32[]{:S(2)}) collective-permute-start(bf16[1,2,256,128]{3,2,1,0:T(8,128)(2,1)S(1)} %get-tuple-element.164), channel_id=1, source_target_pairs={{0,44},{4,40},{8,52},{12,48},{16,60},{20,56},{24,36},{28,32},{32,7... | collective-permute-start | bytes 393224 | tf_op jit(solution)/shard_map/ppermute | solution.py:290
  104.1 35.8 %copy-start.9 = (bf16[1,2,256,128]{3,2,1,0:T(8,128)(2,1)}, bf16[1,2,256,128]{3,2,1,0:T(8,128)(2,1)S(1)}, u32[]{:S(2)}) copy-start(bf16[1,2,256,128]{3,2,1,0:T(8,128)(2,1)S(1)} %collective-permute-done.3.refs_3_) | copy-start | bytes 393220
  104.2 35.7 %copy-start.10 = (bf16[1,2,256,128]{3,2,1,0:T(8,128)(2,1)}, bf16[1,2,256,128]{3,2,1,0:T(8,128)(2,1)S(1)}, u32[]{:S(2)}) copy-start(bf16[1,2,256,128]{3,2,1,0:T(8,128)(2,1)S(1)} %collective-permute-done.2.refs_2_) | copy-start | bytes 393220
  104.2 35.7 %copy-start.11 = (bf16[1,2,256,128]{3,2,1,0:T(8,128)(2,1)}, bf16[1,2,256,128]{3,2,1,0:T(8,128)(2,1)S(1)}, u32[]{:S(2)}) copy-start(bf16[1,2,256,128]{3,2,1,0:T(8,128)(2,1)S(1)} %collective-permute-done.1.refs_1_) | copy-start | bytes 393220
  104.3 35.7 %collective-permute-start.7 = (bf16[1,2,256,128]{3,2,1,0:T(8,128)(2,1)S(1)}, bf16[1,2,256,128]{3,2,1,0:T(8,128)(2,1)S(1)}, u32[]{:S(2)}, u32[]{:S(2)}) collective-permute-start(bf16[1,2,256,128]{3,2,1,0:T(8,128)(2,1)S(1)} %get-tuple-element.157), channel_id=1, source_target_pairs={{0,104},{4,108},{8,112},{12,116},{16,120},{20,124},{24,96},{28,100... | collective-permute-start | bytes 393224 | tf_op jit(solution)/shard_map/ppermute | solution.py:290
  104.7 35.2 %collective-permute-start.6 = (bf16[1,2,256,128]{3,2,1,0:T(8,128)(2,1)S(1)}, bf16[1,2,256,128]{3,2,1,0:T(8,128)(2,1)S(1)}, u32[]{:S(2)}, u32[]{:S(2)}) collective-permute-start(bf16[1,2,256,128]{3,2,1,0:T(8,128)(2,1)S(1)} %get-tuple-element.158), channel_id=1, source_target_pairs={{0,108},{4,104},{8,116},{12,112},{16,124},{20,120},{24,100},{28,96... | collective-permute-start | bytes 393224 | tf_op jit(solution)/shard_map/ppermute | solution.py:290
  109.8 30.2 %collective-permute-start.5 = (bf16[1,2,256,128]{3,2,1,0:T(8,128)(2,1)S(1)}, bf16[1,2,256,128]{3,2,1,0:T(8,128)(2,1)S(1)}, u32[]{:S(2)}, u32[]{:S(2)}) collective-permute-start(bf16[1,2,256,128]{3,2,1,0:T(8,128)(2,1)S(1)} %get-tuple-element.159), channel_id=1, source_target_pairs={{0,56},{4,60},{8,32},{12,36},{16,40},{20,44},{24,48},{28,52},{32,8... | collective-permute-start | bytes 393224 | tf_op jit(solution)/shard_map/ppermute | solution.py:290
  110.6 29.4 %collective-permute-start.4 = (bf16[1,2,256,128]{3,2,1,0:T(8,128)(2,1)S(1)}, bf16[1,2,256,128]{3,2,1,0:T(8,128)(2,1)S(1)}, u32[]{:S(2)}, u32[]{:S(2)}) collective-permute-start(bf16[1,2,256,128]{3,2,1,0:T(8,128)(2,1)S(1)} %get-tuple-element.160), channel_id=1, source_target_pairs={{0,60},{4,56},{8,36},{12,32},{16,44},{20,40},{24,52},{28,48},{32,9... | collective-permute-start | bytes 393224 | tf_op jit(solution)/shard_map/ppermute | solution.py:290
  140.0 36.4 %copy-start.13 = (bf16[1,2,256,128]{3,2,1,0:T(8,128)(2,1)}, bf16[1,2,256,128]{3,2,1,0:T(8,128)(2,1)S(1)}, u32[]{:S(2)}) copy-start(bf16[1,2,256,128]{3,2,1,0:T(8,128)(2,1)S(1)} %collective-permute-done.7.refs_7_) | copy-start | bytes 393220
  140.0 36.4 %copy-start.14 = (bf16[1,2,256,128]{3,2,1,0:T(8,128)(2,1)}, bf16[1,2,256,128]{3,2,1,0:T(8,128)(2,1)S(1)}, u32[]{:S(2)}) copy-start(bf16[1,2,256,128]{3,2,1,0:T(8,128)(2,1)S(1)} %collective-permute-done.6.refs_6_) | copy-start | bytes 393220
  140.0 36.4 %copy-start.15 = (bf16[1,2,256,128]{3,2,1,0:T(8,128)(2,1)}, bf16[1,2,256,128]{3,2,1,0:T(8,128)(2,1)S(1)}, u32[]{:S(2)}) copy-start(bf16[1,2,256,128]{3,2,1,0:T(8,128)(2,1)S(1)} %collective-permute-done.5.refs_5_) | copy-start | bytes 393220
  140.0 36.3 %copy-start.16 = (bf16[1,2,256,128]{3,2,1,0:T(8,128)(2,1)}, bf16[1,2,256,128]{3,2,1,0:T(8,128)(2,1)S(1)}, u32[]{:S(2)}) copy-start(bf16[1,2,256,128]{3,2,1,0:T(8,128)(2,1)S(1)} %collective-permute-done.4.refs_4_) | copy-start | bytes 393220
  140.1 36.3 %collective-permute-start.11 = (bf16[1,2,256,128]{3,2,1,0:T(8,128)(2,1)S(1)}, bf16[1,2,256,128]{3,2,1,0:T(8,128)(2,1)S(1)}, u32[]{:S(2)}, u32[]{:S(2)}) collective-permute-start(bf16[1,2,256,128]{3,2,1,0:T(8,128)(2,1)S(1)} %get-tuple-element.153), channel_id=1, source_target_pairs={{0,16},{4,20},{8,24},{12,28},{16,0},{20,4},{24,8},{28,12},{32,48},... | collective-permute-start | bytes 393224 | tf_op jit(solution)/shard_map/ppermute | solution.py:290
  142.5 33.9 %collective-permute-start.10 = (bf16[1,2,256,128]{3,2,1,0:T(8,128)(2,1)S(1)}, bf16[1,2,256,128]{3,2,1,0:T(8,128)(2,1)S(1)}, u32[]{:S(2)}, u32[]{:S(2)}) collective-permute-start(bf16[1,2,256,128]{3,2,1,0:T(8,128)(2,1)S(1)} %get-tuple-element.154), channel_id=1, source_target_pairs={{0,20},{4,16},{8,28},{12,24},{16,4},{20,0},{24,12},{28,8},{32,52},... | collective-permute-start | bytes 393224 | tf_op jit(solution)/shard_map/ppermute | solution.py:290
  143.6 32.8 %collective-permute-start.9 = (bf16[1,2,256,128]{3,2,1,0:T(8,128)(2,1)S(1)}, bf16[1,2,256,128]{3,2,1,0:T(8,128)(2,1)S(1)}, u32[]{:S(2)}, u32[]{:S(2)}) collective-permute-start(bf16[1,2,256,128]{3,2,1,0:T(8,128)(2,1)S(1)} %get-tuple-element.155), channel_id=1, source_target_pairs={{0,64},{4,68},{8,72},{12,76},{16,80},{20,84},{24,88},{28,92},{32,9... | collective-permute-start | bytes 393224 | tf_op jit(solution)/shard_map/ppermute | solution.py:290
  147.1 29.4 %collective-permute-start.8 = (bf16[1,2,256,128]{3,2,1,0:T(8,128)(2,1)S(1)}, bf16[1,2,256,128]{3,2,1,0:T(8,128)(2,1)S(1)}, u32[]{:S(2)}, u32[]{:S(2)}) collective-permute-start(bf16[1,2,256,128]{3,2,1,0:T(8,128)(2,1)S(1)} %get-tuple-element.156), channel_id=1, source_target_pairs={{0,68},{4,64},{8,76},{12,72},{16,84},{20,80},{24,92},{28,88},{32,1... | collective-permute-start | bytes 393224 | tf_op jit(solution)/shard_map/ppermute | solution.py:290
  176.5 33.7 %collective-permute-start.15 = (bf16[1,2,256,128]{3,2,1,0:T(8,128)(2,1)S(1)}, bf16[1,2,256,128]{3,2,1,0:T(8,128)(2,1)S(1)}, u32[]{:S(2)}, u32[]{:S(2)}) collective-permute-start(bf16[1,2,256,128]{3,2,1,0:T(8,128)(2,1)S(1)} %get-tuple-element.149), channel_id=1, source_target_pairs={{0,96},{4,100},{8,104},{12,108},{16,112},{20,116},{24,120},{28,124... | collective-permute-start | bytes 393224 | tf_op jit(solution)/shard_map/ppermute | solution.py:290
  178.9 31.3 %collective-permute-start.14 = (bf16[1,2,256,128]{3,2,1,0:T(8,128)(2,1)S(1)}, bf16[1,2,256,128]{3,2,1,0:T(8,128)(2,1)S(1)}, u32[]{:S(2)}, u32[]{:S(2)}) collective-permute-start(bf16[1,2,256,128]{3,2,1,0:T(8,128)(2,1)S(1)} %get-tuple-element.150), channel_id=1, source_target_pairs={{0,100},{4,96},{8,108},{12,104},{16,116},{20,112},{24,124},{28,120... | collective-permute-start | bytes 393224 | tf_op jit(solution)/shard_map/ppermute | solution.py:290
  180.1 30.1 %collective-permute-start.13 = (bf16[1,2,256,128]{3,2,1,0:T(8,128)(2,1)S(1)}, bf16[1,2,256,128]{3,2,1,0:T(8,128)(2,1)S(1)}, u32[]{:S(2)}, u32[]{:S(2)}) collective-permute-start(bf16[1,2,256,128]{3,2,1,0:T(8,128)(2,1)S(1)} %get-tuple-element.151), channel_id=1, source_target_pairs={{0,32},{4,36},{8,40},{12,44},{16,48},{20,52},{24,56},{28,60},{32,6... | collective-permute-start | bytes 393224 | tf_op jit(solution)/shard_map/ppermute | solution.py:290
  181.1 29.2 %collective-permute-start.12 = (bf16[1,2,256,128]{3,2,1,0:T(8,128)(2,1)S(1)}, bf16[1,2,256,128]{3,2,1,0:T(8,128)(2,1)S(1)}, u32[]{:S(2)}, u32[]{:S(2)}) collective-permute-start(bf16[1,2,256,128]{3,2,1,0:T(8,128)(2,1)S(1)} %get-tuple-element.152), channel_id=1, source_target_pairs={{0,36},{4,32},{8,44},{12,40},{16,52},{20,48},{24,60},{28,56},{32,6... | collective-permute-start | bytes 393224 | tf_op jit(solution)/shard_map/ppermute | solution.py:290
  210.3 33.3 %collective-permute-start.19 = (bf16[1,2,256,128]{3,2,1,0:T(8,128)(2,1)S(1)}, bf16[1,2,256,128]{3,2,1,0:T(8,128)(2,1)S(1)}, u32[]{:S(2)}, u32[]{:S(2)}) collective-permute-start(bf16[1,2,256,128]{3,2,1,0:T(8,128)(2,1)S(1)} %get-tuple-element.145), channel_id=1, source_target_pairs={{0,24},{4,28},{8,0},{12,4},{16,8},{20,12},{24,16},{28,20},{32,56},... | collective-permute-start | bytes 393224 | tf_op jit(solution)/shard_map/ppermute | solution.py:290
  212.5 31.2 %collective-permute-start.18 = (bf16[1,2,256,128]{3,2,1,0:T(8,128)(2,1)S(1)}, bf16[1,2,256,128]{3,2,1,0:T(8,128)(2,1)S(1)}, u32[]{:S(2)}, u32[]{:S(2)}) collective-permute-start(bf16[1,2,256,128]{3,2,1,0:T(8,128)(2,1)S(1)} %get-tuple-element.146), channel_id=1, source_target_pairs={{0,28},{4,24},{8,4},{12,0},{16,12},{20,8},{24,20},{28,16},{32,60},... | collective-permute-start | bytes 393224 | tf_op jit(solution)/shard_map/ppermute | solution.py:290
  213.6 30.1 %collective-permute-start.17 = (bf16[1,2,256,128]{3,2,1,0:T(8,128)(2,1)S(1)}, bf16[1,2,256,128]{3,2,1,0:T(8,128)(2,1)S(1)}, u32[]{:S(2)}, u32[]{:S(2)}) collective-permute-start(bf16[1,2,256,128]{3,2,1,0:T(8,128)(2,1)S(1)} %get-tuple-element.147), channel_id=1, source_target_pairs={{0,8},{4,12},{8,16},{12,20},{16,24},{20,28},{24,0},{28,4},{32,40},... | collective-permute-start | bytes 393224 | tf_op jit(solution)/shard_map/ppermute | solution.py:290
  214.6 29.1 %collective-permute-start.16 = (bf16[1,2,256,128]{3,2,1,0:T(8,128)(2,1)S(1)}, bf16[1,2,256,128]{3,2,1,0:T(8,128)(2,1)S(1)}, u32[]{:S(2)}, u32[]{:S(2)}) collective-permute-start(bf16[1,2,256,128]{3,2,1,0:T(8,128)(2,1)S(1)} %get-tuple-element.148), channel_id=1, source_target_pairs={{0,12},{4,8},{8,20},{12,16},{16,28},{20,24},{24,4},{28,0},{32,44},... | collective-permute-start | bytes 393224 | tf_op jit(solution)/shard_map/ppermute | solution.py:290
  243.7 39.2 %copy-start.25 = (bf16[1,2,256,128]{3,2,1,0:T(8,128)(2,1)}, bf16[1,2,256,128]{3,2,1,0:T(8,128)(2,1)S(1)}, u32[]{:S(2)}) copy-start(bf16[1,2,256,128]{3,2,1,0:T(8,128)(2,1)S(1)} %collective-permute-done.19.refs_19_) | copy-start | bytes 393220
  243.7 39.2 %copy-start.26 = (bf16[1,2,256,128]{3,2,1,0:T(8,128)(2,1)}, bf16[1,2,256,128]{3,2,1,0:T(8,128)(2,1)S(1)}, u32[]{:S(2)}) copy-start(bf16[1,2,256,128]{3,2,1,0:T(8,128)(2,1)S(1)} %collective-permute-done.18.refs_18_) | copy-start | bytes 393220
  243.7 39.2 %copy-start.27 = (bf16[1,2,256,128]{3,2,1,0:T(8,128)(2,1)}, bf16[1,2,256,128]{3,2,1,0:T(8,128)(2,1)S(1)}, u32[]{:S(2)}) copy-start(bf16[1,2,256,128]{3,2,1,0:T(8,128)(2,1)S(1)} %collective-permute-done.17.refs_17_) | copy-start | bytes 393220
  243.7 39.1 %copy-start.28 = (bf16[1,2,256,128]{3,2,1,0:T(8,128)(2,1)}, bf16[1,2,256,128]{3,2,1,0:T(8,128)(2,1)S(1)}, u32[]{:S(2)}) copy-start(bf16[1,2,256,128]{3,2,1,0:T(8,128)(2,1)S(1)} %collective-permute-done.16.refs_16_) | copy-start | bytes 393220
  243.8 39.1 %collective-permute-start.23 = (bf16[1,2,256,128]{3,2,1,0:T(8,128)(2,1)S(1)}, bf16[1,2,256,128]{3,2,1,0:T(8,128)(2,1)S(1)}, u32[]{:S(2)}, u32[]{:S(2)}) collective-permute-start(bf16[1,2,256,128]{3,2,1,0:T(8,128)(2,1)S(1)} %get-tuple-element.141), channel_id=1, source_target_pairs={{0,88},{4,92},{8,64},{12,68},{16,72},{20,76},{24,80},{28,84},{32,1... | collective-permute-start | bytes 393224 | tf_op jit(solution)/shard_map/ppermute | solution.py:290
  248.8 34.1 %collective-permute-start.22 = (bf16[1,2,256,128]{3,2,1,0:T(8,128)(2,1)S(1)}, bf16[1,2,256,128]{3,2,1,0:T(8,128)(2,1)S(1)}, u32[]{:S(2)}, u32[]{:S(2)}) collective-permute-start(bf16[1,2,256,128]{3,2,1,0:T(8,128)(2,1)S(1)} %get-tuple-element.142), channel_id=1, source_target_pairs={{0,92},{4,88},{8,68},{12,64},{16,76},{20,72},{24,84},{28,80},{32,1... | collective-permute-start | bytes 393224 | tf_op jit(solution)/shard_map/ppermute | solution.py:290
  249.9 33.0 %collective-permute-start.21 = (bf16[1,2,256,128]{3,2,1,0:T(8,128)(2,1)S(1)}, bf16[1,2,256,128]{3,2,1,0:T(8,128)(2,1)S(1)}, u32[]{:S(2)}, u32[]{:S(2)}) collective-permute-start(bf16[1,2,256,128]{3,2,1,0:T(8,128)(2,1)S(1)} %get-tuple-element.143), channel_id=1, source_target_pairs={{0,72},{4,76},{8,80},{12,84},{16,88},{20,92},{24,64},{28,68},{32,1... | collective-permute-start | bytes 393224 | tf_op jit(solution)/shard_map/ppermute | solution.py:290
  253.5 29.4 %collective-permute-start.20 = (bf16[1,2,256,128]{3,2,1,0:T(8,128)(2,1)S(1)}, bf16[1,2,256,128]{3,2,1,0:T(8,128)(2,1)S(1)}, u32[]{:S(2)}, u32[]{:S(2)}) collective-permute-start(bf16[1,2,256,128]{3,2,1,0:T(8,128)(2,1)S(1)} %get-tuple-element.144), channel_id=1, source_target_pairs={{0,76},{4,72},{8,84},{12,80},{16,92},{20,88},{24,68},{28,64},{32,1... | collective-permute-start | bytes 393224 | tf_op jit(solution)/shard_map/ppermute | solution.py:290
  282.9 38.7 %copy-start.29 = (bf16[1,2,256,128]{3,2,1,0:T(8,128)(2,1)}, bf16[1,2,256,128]{3,2,1,0:T(8,128)(2,1)S(1)}, u32[]{:S(2)}) copy-start(bf16[1,2,256,128]{3,2,1,0:T(8,128)(2,1)S(1)} %collective-permute-done.23.refs_23_) | copy-start | bytes 393220
  282.9 38.6 %copy-start.30 = (bf16[1,2,256,128]{3,2,1,0:T(8,128)(2,1)}, bf16[1,2,256,128]{3,2,1,0:T(8,128)(2,1)S(1)}, u32[]{:S(2)}) copy-start(bf16[1,2,256,128]{3,2,1,0:T(8,128)(2,1)S(1)} %collective-permute-done.22.refs_22_) | copy-start | bytes 393220
  282.9 38.6 %copy-start.31 = (bf16[1,2,256,128]{3,2,1,0:T(8,128)(2,1)}, bf16[1,2,256,128]{3,2,1,0:T(8,128)(2,1)S(1)}, u32[]{:S(2)}) copy-start(bf16[1,2,256,128]{3,2,1,0:T(8,128)(2,1)S(1)} %collective-permute-done.21.refs_21_) | copy-start | bytes 393220
  282.9 38.6 %copy-start.32 = (bf16[1,2,256,128]{3,2,1,0:T(8,128)(2,1)}, bf16[1,2,256,128]{3,2,1,0:T(8,128)(2,1)S(1)}, u32[]{:S(2)}) copy-start(bf16[1,2,256,128]{3,2,1,0:T(8,128)(2,1)S(1)} %collective-permute-done.20.refs_20_) | copy-start | bytes 393220
  283.0 38.6 %collective-permute-start.27 = (bf16[1,2,256,128]{3,2,1,0:T(8,128)(2,1)S(1)}, bf16[1,2,256,128]{3,2,1,0:T(8,128)(2,1)S(1)}, u32[]{:S(2)}, u32[]{:S(2)}) collective-permute-start(bf16[1,2,256,128]{3,2,1,0:T(8,128)(2,1)S(1)} %get-tuple-element.137), channel_id=1, source_target_pairs={{0,112},{4,116},{8,120},{12,124},{16,96},{20,100},{24,104},{28,108... | collective-permute-start | bytes 393224 | tf_op jit(solution)/shard_map/ppermute | solution.py:290
  287.9 33.7 %collective-permute-start.26 = (bf16[1,2,256,128]{3,2,1,0:T(8,128)(2,1)S(1)}, bf16[1,2,256,128]{3,2,1,0:T(8,128)(2,1)S(1)}, u32[]{:S(2)}, u32[]{:S(2)}) collective-permute-start(bf16[1,2,256,128]{3,2,1,0:T(8,128)(2,1)S(1)} %get-tuple-element.138), channel_id=1, source_target_pairs={{0,116},{4,112},{8,124},{12,120},{16,100},{20,96},{24,108},{28,104... | collective-permute-start | bytes 393224 | tf_op jit(solution)/shard_map/ppermute | solution.py:290
  288.4 33.2 %collective-permute-start.25 = (bf16[1,2,256,128]{3,2,1,0:T(8,128)(2,1)S(1)}, bf16[1,2,256,128]{3,2,1,0:T(8,128)(2,1)S(1)}, u32[]{:S(2)}, u32[]{:S(2)}) collective-permute-start(bf16[1,2,256,128]{3,2,1,0:T(8,128)(2,1)S(1)} %get-tuple-element.139), channel_id=1, source_target_pairs={{0,48},{4,52},{8,56},{12,60},{16,32},{20,36},{24,40},{28,44},{32,8... | collective-permute-start | bytes 393224 | tf_op jit(solution)/shard_map/ppermute | solution.py:290
  292.5 29.2 %collective-permute-start.24 = (bf16[1,2,256,128]{3,2,1,0:T(8,128)(2,1)S(1)}, bf16[1,2,256,128]{3,2,1,0:T(8,128)(2,1)S(1)}, u32[]{:S(2)}, u32[]{:S(2)}) collective-permute-start(bf16[1,2,256,128]{3,2,1,0:T(8,128)(2,1)S(1)} %get-tuple-element.140), channel_id=1, source_target_pairs={{0,52},{4,48},{8,60},{12,56},{16,36},{20,32},{24,44},{28,40},{32,8... | collective-permute-start | bytes 393224 | tf_op jit(solution)/shard_map/ppermute | solution.py:290
  292.5 36.0 %copy-start.40 = (s32[1,32]{1,0:T(1,128)S(1)}, s32[1,32]{1,0:T(1,128)}, u32[]{:S(2)}) copy-start(s32[1,32]{1,0:T(1,128)} %constant.207) | copy-start | bytes 388
  292.5 36.0 %copy-start.41 = (s32[1,32]{1,0:T(1,128)S(1)}, s32[1,32]{1,0:T(1,128)}, u32[]{:S(2)}) copy-start(s32[1,32]{1,0:T(1,128)} %constant.205) | copy-start | bytes 388
  322.4 6.6 %collective-permute-start.30 = (bf16[1,2,256,128]{3,2,1,0:T(8,128)(2,1)S(1)}, bf16[1,2,256,128]{3,2,1,0:T(8,128)(2,1)S(1)}, u32[]{:S(2)}, u32[]{:S(2)}) collective-permute-start(bf16[1,2,256,128]{3,2,1,0:T(8,128)(2,1)S(1)} %get-tuple-element.134), channel_id=1, source_target_pairs={{0,4},{4,0},{8,12},{12,8},{16,20},{20,16},{24,28},{28,24},{32,36},... | collective-permute-start | bytes 393224 | tf_op jit(solution)/shard_map/ppermute | solution.py:290
  322.9 9.0 %collective-permute-start.29 = (bf16[1,2,256,128]{3,2,1,0:T(8,128)(2,1)S(1)}, bf16[1,2,256,128]{3,2,1,0:T(8,128)(2,1)S(1)}, u32[]{:S(2)}, u32[]{:S(2)}) collective-permute-start(bf16[1,2,256,128]{3,2,1,0:T(8,128)(2,1)S(1)} %get-tuple-element.135), channel_id=1, source_target_pairs={{0,80},{4,84},{8,88},{12,92},{16,64},{20,68},{24,72},{28,76},{32,1... | collective-permute-start | bytes 393224 | tf_op jit(solution)/shard_map/ppermute | solution.py:290
  328.2 9.3 %collective-permute-start.28 = (bf16[1,2,256,128]{3,2,1,0:T(8,128)(2,1)S(1)}, bf16[1,2,256,128]{3,2,1,0:T(8,128)(2,1)S(1)}, u32[]{:S(2)}, u32[]{:S(2)}) collective-permute-start(bf16[1,2,256,128]{3,2,1,0:T(8,128)(2,1)S(1)} %get-tuple-element.136), channel_id=1, source_target_pairs={{0,84},{4,80},{8,92},{12,88},{16,68},{20,64},{24,76},{28,72},{32,1... | collective-permute-start | bytes 393224 | tf_op jit(solution)/shard_map/ppermute | solution.py:290
  (25 other events, 500.9 us)

commit v3 on v2

v3 whole, which is shorter than its diff:
```python
import functools

import jax
import jax.numpy as jnp
from jax import lax
from jax.experimental import pallas as pl
from jax.experimental.pallas import tpu as pltpu
from jax.sharding import PartitionSpec as P

F32 = jnp.float32
BF16 = jnp.bfloat16
LOG2E = 1.4426950408889634
DEAD = -1e9
NT = (((1,), (1,)), ((), ()))


def normalise(values_in):
    centre = values_in - jnp.mean(values_in, -1, keepdims=True)
    spread = jnp.mean(centre * centre, -1, keepdims=True)
    return centre * lax.rsqrt(spread + 1e-05)


def bias_kernel(x_hbm, wb_ref, normed_hbm, bias_ref, x_ref, normed_ref, hold_ref, in_sems, out_sems):
    rows = x_ref.shape[0]
    heads = bias_ref.shape[0]
    parts = in_sems.shape[0]
    span = rows // parts

    def fetch(p):
        part = pl.ds(p * span, span)
        return pltpu.make_async_copy(x_hbm.at[part], x_ref.at[part], in_sems.at[p])

    def store(p):
        part = pl.ds(p * span, span)
        return pltpu.make_async_copy(normed_ref.at[part], normed_hbm.at[part], out_sems.at[p])

    for p in range(parts):
        fetch(p).start()
    for p in range(parts):
        fetch(p).wait()
        for r in range(p * span, (p + 1) * span):
            normed = normalise(x_ref[r].astype(F32)).astype(BF16)
            normed_ref[r] = normed
            res = lax.dot_general(wb_ref[...], normed, NT, preferred_element_type=F32)
            for h in range(heads):
                hold_ref[h, r : r + 1, :] = res[h : h + 1]
        store(p).start()
    bias_ref[...] = hold_ref[...].astype(BF16)
    for p in range(parts):
        store(p).wait()


def local_bias(local, w_bias):
    rows, width, chans = local.shape
    heads = w_bias.shape[1]
    wb = jnp.pad(w_bias.T, ((0, 8 - heads), (0, 0)))
    vmem = pl.BlockSpec(memory_space=pltpu.VMEM)
    hbm = pl.BlockSpec(memory_space=pltpu.HBM)
    return pl.pallas_call(
        bias_kernel,
        name="bias",
        in_specs=[hbm, vmem],
        out_specs=[hbm, vmem],
        out_shape=[
            jax.ShapeDtypeStruct((rows, width, chans), BF16),
            jax.ShapeDtypeStruct((heads, rows, width), BF16),
        ],
        scratch_shapes=[
            pltpu.VMEM((rows, width, chans), BF16),
            pltpu.VMEM((rows, width, chans), BF16),
            pltpu.VMEM((heads, rows, width), F32),
            pltpu.SemaphoreType.DMA((8,)),
            pltpu.SemaphoreType.DMA((8,)),
        ],
        compiler_params=pltpu.CompilerParams(vmem_limit_bytes=24 * 1024 * 1024),
    )(local, wb)


def masked_bias(bias, length):
    live = jnp.arange(bias.shape[-1], dtype=jnp.int32) < length
    return jnp.where(live, bias.astype(F32) * LOG2E, DEAD)


def update_kernel(
    groups_ref,
    lengths_ref,
    info_ref,
    x_hbm,
    n_hbm,
    bias_ref,
    wp_ref,
    wo_ref,
    wu_ref,
    wd_ref,
    out_ref,
    order_s,
    x_s,
    n_s,
    mid_s,
    sum_s,
    low_s,
    high_s,
    sems,
):
    count, rows, width, chans = out_ref.shape
    heads = bias_ref.shape[0]
    inner = wp_ref.shape[1] // 4
    size_h = inner // heads
    group = info_ref[0]
    row_base = info_ref[1]
    length = lengths_ref[group]
    lane = lax.broadcasted_iota(jnp.int32, (width, inner), 1)
    zero = jnp.zeros((), BF16)

    for b in range(count):
        order_s[groups_ref[group, b]] = b

    def fetches(i, slot):
        part = order_s[i]
        return (
            pltpu.make_async_copy(x_hbm.at[part], x_s.at[slot], sems.at[0, slot]),
            pltpu.make_async_copy(n_hbm.at[part], n_s.at[slot], sems.at[1, slot]),
        )

    def head_mask(h):
        return (lane >= h * size_h) & (lane < (h + 1) * size_h)

    masks = [head_mask(h) for h in range(heads)]

    def project(normed):
        proj = jnp.dot(normed, wp_ref[...], preferred_element_type=F32)
        query = (proj[:, :inner] * (size_h ** (-0.5) * LOG2E)).astype(BF16)
        keys = proj[:, inner : 2 * inner].astype(BF16)
        values = proj[:, 2 * inner : 3 * inner].astype(BF16)
        return query, keys, jnp.concatenate([values, jnp.ones_like(values)], 1), proj[:, 3 * inner :]

    def score_of(query, keys, mask, h):
        score = lax.dot_general(jnp.where(mask, query, zero), keys, NT, preferred_element_type=F32)
        return score + bias_ref[h]

    def weigh(score, side):
        return jnp.dot(jnp.exp2(score).astype(BF16), side, preferred_element_type=F32)

    def gated_of(both, gate):
        return (jax.nn.sigmoid(gate) * (both[:, :inner] / both[:, inner:])).astype(BF16)

    def close(before, first, gated):
        update = jnp.dot(gated, wo_ref[...], preferred_element_type=F32)
        place = lax.broadcasted_iota(jnp.int32, update.shape, 0)
        live = (place % width < length) & (first + place // width < length)
        middle = before.astype(F32) + jnp.where(live, update, 0.0)
        return middle.astype(BF16)

    def finish(middle):
        middle = middle.astype(F32)
        normed_mid = normalise(middle).astype(BF16)
        hidden = jnp.dot(normed_mid, wu_ref[...], preferred_element_type=F32)
        hidden = jax.nn.relu(hidden).astype(BF16)
        down = jnp.dot(hidden, wd_ref[...], preferred_element_type=F32)
        return (middle + down).astype(BF16)

    def store(i, updated):
        out_ref[i] = updated.reshape(rows, width, chans)

    def attend(i, slot, first):
        past = mid_s[...]
        query, keys, side, gate = project(n_s[slot].reshape(rows * width, chans))
        ends = []
        for r in range(rows):
            at = slice(r * width, (r + 1) * width)
            both = None
            for h in range(heads):
                each = weigh(score_of(query[at], keys[at], masks[h], h), side[at])
                mask = jnp.concatenate([masks[h], masks[h]], 1)
                both = each if both is None else jnp.where(mask, each, both)
            ends.append(both)
        gated = gated_of(jnp.concatenate(ends, 0), gate)
        store(jnp.maximum(i - 1, 0), finish(past))
        mid_s[...] = close(x_s[slot].reshape(rows * width, chans), first, gated)
        low = functools.reduce(jnp.minimum, [e[:, inner:] for e in ends])
        high = functools.reduce(jnp.maximum, [e[:, inner:] for e in ends])
        low_s[...] = jnp.minimum(low_s[...], jnp.min(low.reshape(-1, 8, inner), 0))
        high_s[...] = jnp.maximum(high_s[...], jnp.max(high.reshape(-1, 8, inner), 0))

    low_s[...] = jnp.ones_like(low_s)
    high_s[...] = jnp.ones_like(high_s)
    mid_s[...] = jnp.zeros_like(mid_s)
    for copy in fetches(0, 0):
        copy.start()

    def one_block(i, carry):
        slot = lax.rem(i, 2)
        first = row_base + order_s[i] * rows

        @pl.when(i + 1 < count)
        def _():
            for copy in fetches(i + 1, 1 - slot):
                copy.start()

        for copy in fetches(i, slot):
            copy.wait()

        @pl.when(first < length)
        def _():
            attend(i, slot, first)

        @pl.when(first >= length)
        def _():
            store(jnp.maximum(i - 1, 0), finish(mid_s[...]))
            mid_s[...] = x_s[slot].reshape(rows * width, chans)

        return carry

    lax.fori_loop(0, count, one_block, 0)
    store(count - 1, finish(mid_s[...]))
    good = (jnp.min(low_s[...]) > 1e-20) & (jnp.max(high_s[...]) < 1e30)

    @pl.when(jnp.logical_not(good))
    def _():
        def again(i, carry):
            first = row_base + order_s[i] * rows

            @pl.when(first < length)
            def _():
                for copy in fetches(i, 0):
                    copy.start()
                for copy in fetches(i, 0):
                    copy.wait()

                def one_row(r, carry):
                    query, keys, side, gate = project(n_s[0, r])

                    def one_head(h, carry):
                        mask = head_mask(h)
                        score = score_of(query, keys, mask, h)
                        each = weigh(score - jnp.max(score, -1, keepdims=True), side)
                        sum_s[...] = jnp.where(jnp.concatenate([mask, mask], 1), each, sum_s[...])
                        return carry

                    lax.fori_loop(0, heads, one_head, 0)
                    gated = gated_of(sum_s[...], gate)
                    out_ref[i, r] = finish(close(x_s[0, r], first + r, gated))
                    return carry

                lax.fori_loop(0, rows, one_row, 0)

            return carry

        lax.fori_loop(0, count, again, 0)


def update_blocks(groups, lengths, info, blocks, normeds, bias, w_proj, w_out, w_up, w_down):
    count, rows, width, chans = blocks.shape
    inner = w_proj.shape[1] // 4
    vmem = pl.BlockSpec(memory_space=pltpu.VMEM)
    smem = pl.BlockSpec(memory_space=pltpu.SMEM)
    hbm = pl.BlockSpec(memory_space=pltpu.HBM)
    return pl.pallas_call(
        update_kernel,
        name="update",
        in_specs=[smem, smem, smem, hbm, hbm] + [vmem] * 5,
        out_specs=vmem,
        out_shape=jax.ShapeDtypeStruct((count, rows, width, chans), BF16),
        scratch_shapes=[
            pltpu.SMEM((count,), jnp.int32),
            pltpu.VMEM((2, rows, width, chans), BF16),
            pltpu.VMEM((2, rows, width, chans), BF16),
            pltpu.VMEM((rows * width, chans), BF16),
            pltpu.VMEM((width, 2 * inner), F32),
            pltpu.VMEM((8, inner), F32),
            pltpu.VMEM((8, inner), F32),
            pltpu.SemaphoreType.DMA((2, 2)),
        ],
        compiler_params=pltpu.CompilerParams(vmem_limit_bytes=24 * 1024 * 1024),
    )(groups, lengths, info, blocks, normeds, bias, w_proj, w_out, w_up, w_down)


def shards(pair, lengths, block_group, w_proj, w_bias, w_out, w_up, w_down):
    group_idx = lax.axis_index("sample")
    axial_idx = lax.axis_index("axial")
    groups_n = lax.axis_size("sample")
    _, ax_rows, width, chans = pair.shape
    blk_rows = ax_rows // groups_n
    local = pair[0]
    info = jnp.stack([group_idx, axial_idx * ax_rows]).astype(jnp.int32)
    normed, bias = local_bias(local, w_bias)
    length = jnp.take(lengths, group_idx)
    crop_bias = masked_bias(lax.all_gather(bias, "axial", axis=1, tiled=True), length)
    shape = (groups_n, blk_rows, width, chans)
    updated = update_blocks(
        block_group,
        lengths,
        info,
        local.reshape(shape),
        normed.reshape(shape),
        crop_bias,
        w_proj,
        w_out,
        w_up,
        w_down,
    )
    arrived = lax.all_to_all(updated, "sample", split_axis=0, concat_axis=0, tiled=True)
    return arrived.reshape(1, 1, groups_n, blk_rows, width, chans)


def solution(mesh):
    return jax.shard_map(
        shards,
        mesh=mesh,
        in_specs=(P("sample", "axial", None, None), P(), P(), P(), P(), P(), P(), P()),
        out_specs=P("sample", "axial", None, None, None, None),
        check_vma=False,
    )
```

time: 475 us -> 326 us (0.69); the launches traced: 468 us -> 325 us
  Pallas kernels: 369 us -> 239 us
  blocking collectives: 13.4 us -> 73 us
  starting transfers between devices: 57.7 us -> 0 us
  waiting for transfers between devices: 8.52 us -> 0 us
    pallas_call x10 -> x2, Pallas kernels: 369 us -> 239 us  [the longest x1 231 us: update_blocks(): pl.pallas_call(update_kernel, name='update', in_specs=[smem, smem, smem,...]
    all_to_all x0 -> x1, blocking collectives: none -> 59.6 us  [shards(): lax.all_to_all(updated, 'sample', split_axis=0, concat_axis=0, tiled=True)]
    ppermute x31 -> x0, starting transfers between devices: 57.7 us -> none  [shards(): part = lax.ppermute(part, 'sample', pairs)]
    ppermute x31 -> x0, waiting for transfers between devices: 8.52 us -> none  [shards(): part = lax.ppermute(part, 'sample', pairs)]
    unnamed x84 -> x21, local copies, waits for them, and re-layouts: 11.3 us -> 10.6 us
  transfers between devices with their start and end apart: 31 -> 0, of which waited for: 2 -> 0; matrix products, arithmetic and copies ran while one was open for 0% -> 0% of each run, Pallas kernels for 44% -> 0%
where the time goes in v3:
time: 326 us; the launch traced here: 325 us
  Pallas kernels  239 us (73%)
  blocking collectives  73 us (22%)
  local copies, waits for them, and re-layouts  12.7 us (4%)
    pallas_call x1, Pallas kernels, update_blocks(): pl.pallas_call(update_kernel, name='update', in_specs=[smem, smem, smem,...  231 us
    all_to_all x1, blocking collectives, shards(): lax.all_to_all(updated, 'sample', split_axis=0, concat_axis=0, tiled=True)  59.6 us
    all_gather x1, blocking collectives, shards(): lax.all_gather(bias, 'axial', axis=1, tiled=True)  13.4 us
    unnamed x21, local copies, waits for them, and re-layouts  10.6 us
    pallas_call x1, Pallas kernels, local_bias(): pl.pallas_call(bias_kernel, name='bias', in_specs=[hbm, vmem], out_specs=...  8.02 us

profile of v3, /device:TPU:1, one launch (start us, length us, event | category | flops | bytes accessed | tf_op | source)
XLA Modules:
  0.0 325.2 jit_solution(10152131897916017420)
XLA Ops:
  0.0 0.0 copy-start.9
  0.0 0.0 copy-start.7
  0.0 1.4 dynamic-slice.2
  2.0 0.7 pad.4.wb_ref
  2.7 0.0 copy-start
  2.7 2.2 copy-done
  4.9 0.0 copy-start.4
  4.9 0.0 copy-start.5
  4.9 0.0 copy-start.6
  4.9 0.0 copy-start.8
  4.9 8.0 %bias.1 = (bf16[64,256,128]{2,1,0:T(8,128)(2,1)S(1)}, bf16[4,64,256]{2,1,0:T(8,128)(2,1)S(1)}) custom-call(bf16[64,256,128]{2,1,0:T(8,128)(2,1)S(1)} %bitcast.9, bf16[8,128]{1,0:T(8,128)(2,1)S(1)} %pad.4.wb_ref), custom_call_target="tpu_custom_call" | custom-call | tf_op jit(solution)/shard_map/bias/pallas_call | solution.py:59
  12.9 0.0 copy-start.2
  12.9 2.0 copy-done.2
  14.9 13.4 %all_gather.3 = bf16[4,256,256]{2,1,0:T(8,128)(2,1)S(1)} all-gather(bf16[4,64,256]{2,1,0:T(8,128)(2,1)S(1)} %get-tuple-element.8), channel_id=1, replica_groups=mesh['sample'=32,'axial'=4] {'axial'}, dimensions={1}, use_global_device_ids=true | all-gather | bytes 655360 | tf_op jit(solution)/shard_map/all_gather | solution.py:288
  28.3 0.1 pad_add_fusion.info_ref
  28.4 0.1 multiply_select_fusion.bias_ref
  28.5 0.0 copy-done.9
  28.6 0.0 copy-done.7
  28.6 0.0 copy-done.4
  28.6 0.0 copy-done.5
  28.6 0.0 copy-done.6
  28.6 0.0 copy-done.8
  28.6 0.0 copy-start.1
  28.6 2.2 copy-done.1
  30.8 0.0 copy-start.3
  30.8 2.2 copy-done.3
  33.0 230.6 %update.1 = bf16[32,2,256,128]{3,2,1,0:T(8,128)(2,1)S(1)} custom-call(s32[32,32]{1,0:T(8,128)S(1)} %copy-done.8, s32[32]{0:T(128)S(1)} %copy-done.9, s32[2]{0:T(128)S(1)} %pad_add_fusion.info_ref, bf16[32,2,256,128]{3,2,1,0:T(8,128)(2,1)S(1)} %bitcast.10, bf16[32,2,256,128]{3,2,1,0:T(8,128)(2,1)S(1)} %bitcast.11, ...), custom_call_target="tpu_custom_call" | custom-call | tf_op jit(solution)/shard_map/update/pallas_call | solution.py:258
  263.6 59.6 %all_to_all.5 = bf16[32,2,256,128]{3,2,1,0:T(8,128)(2,1)S(1)} all-to-all(bf16[32,2,256,128]{3,2,1,0:T(8,128)(2,1)S(1)} %update.1), channel_id=1, replica_groups=mesh['sample'=32,'axial'=4] {'sample'}, dimensions={0} | all-to-all | bytes 8388608 | tf_op jit(solution)/shard_map/all_to_all | solution.py:302
  323.2 2.0 copy.10
  (1 shorter events, 0.0 us)
Async XLA Ops:
  0.0 28.5 %copy-start.9 = (s32[32]{0:T(128)S(1)}, s32[32]{0:T(128)}, u32[]{:S(2)}) copy-start(s32[32]{0:T(128)} %lengths_ref.1) | copy-start | bytes 388
  0.0 28.6 %copy-start.7 = (bf16[128,128]{1,0:T(8,128)(2,1)S(1)}, bf16[128,128]{1,0:T(8,128)(2,1)}, u32[]{:S(2)}) copy-start(bf16[128,128]{1,0:T(8,128)(2,1)} %wo_ref.1) | copy-start | bytes 98308
  2.7 2.2 copy-start
  4.9 23.7 %copy-start.4 = (bf16[128,512]{1,0:T(8,128)(2,1)S(1)}, bf16[128,512]{1,0:T(8,128)(2,1)}, u32[]{:S(2)}) copy-start(bf16[128,512]{1,0:T(8,128)(2,1)} %wp_ref.1) | copy-start | bytes 393220
  4.9 23.7 %copy-start.5 = (bf16[128,512]{1,0:T(8,128)(2,1)S(1)}, bf16[128,512]{1,0:T(8,128)(2,1)}, u32[]{:S(2)}) copy-start(bf16[128,512]{1,0:T(8,128)(2,1)} %wu_ref.1) | copy-start | bytes 393220
  4.9 23.7 %copy-start.6 = (bf16[512,128]{1,0:T(8,128)(2,1)S(1)}, bf16[512,128]{1,0:T(8,128)(2,1)}, u32[]{:S(2)}) copy-start(bf16[512,128]{1,0:T(8,128)(2,1)} %wd_ref.1) | copy-start | bytes 393220
  4.9 23.7 %copy-start.8 = (s32[32,32]{1,0:T(8,128)S(1)}, s32[32,32]{1,0:T(8,128)}, u32[]{:S(2)}) copy-start(s32[32,32]{1,0:T(8,128)} %groups_ref.1) | copy-start | bytes 12292
  12.9 2.0 copy-start.2
  28.6 2.2 copy-start.1
  30.8 2.2 copy-start.3

commit v4 on v3

--- a/solution.py
+++ b/solution.py
@@ -72,13 +72,8 @@
             pltpu.SemaphoreType.DMA((8,)),
             pltpu.SemaphoreType.DMA((8,)),
         ],
-        compiler_params=pltpu.CompilerParams(vmem_limit_bytes=24 * 1024 * 1024),
+        compiler_params=pltpu.CompilerParams(vmem_limit_bytes=61 * 1024 * 1024),
     )(local, wb)
-
-
-def masked_bias(bias, length):
-    live = jnp.arange(bias.shape[-1], dtype=jnp.int32) < length
-    return jnp.where(live, bias.astype(F32) * LOG2E, DEAD)
 
 
 def update_kernel(
@@ -94,6 +89,7 @@
     wd_ref,
     out_ref,
     order_s,
+    bias_s,
     x_s,
     n_s,
     mid_s,
@@ -103,6 +99,9 @@
     sems,
 ):
     count, rows, width, chans = out_ref.shape
+    per = x_s.shape[1]
+    steps = count // per
+    span = per * rows * width
     heads = bias_ref.shape[0]
     inner = wp_ref.shape[1] // 4
     size_h = inner // heads
@@ -112,15 +111,23 @@
     lane = lax.broadcasted_iota(jnp.int32, (width, inner), 1)
     zero = jnp.zeros((), BF16)
 
+    keys_live = lax.broadcasted_iota(jnp.int32, (width, width), 1) < length
+
     for b in range(count):
         order_s[groups_ref[group, b]] = b
 
     def fetches(i, slot):
-        part = order_s[i]
-        return (
-            pltpu.make_async_copy(x_hbm.at[part], x_s.at[slot], sems.at[0, slot]),
-            pltpu.make_async_copy(n_hbm.at[part], n_s.at[slot], sems.at[1, slot]),
-        )
+        copies = []
+        for p in range(per):
+            part = order_s[i * per + p]
+            copies += [
+                pltpu.make_async_copy(x_hbm.at[part], x_s.at[slot, p], sems.at[0, p, slot]),
+                pltpu.make_async_copy(n_hbm.at[part], n_s.at[slot, p], sems.at[1, p, slot]),
+            ]
+        return copies
+
+    def firsts(i):
+        return [row_base + order_s[i * per + p] * rows for p in range(per)]
 
     def head_mask(h):
         return (lane >= h * size_h) & (lane < (h + 1) * size_h)
@@ -136,7 +143,7 @@
 
     def score_of(query, keys, mask, h):
         score = lax.dot_general(jnp.where(mask, query, zero), keys, NT, preferred_element_type=F32)
-        return score + bias_ref[h]
+        return score + bias_s[h]
 
     def weigh(score, side):
         return jnp.dot(jnp.exp2(score).astype(BF16), side, preferred_element_type=F32)
@@ -146,10 +153,14 @@
 
     def close(before, first, gated):
         update = jnp.dot(gated, wo_ref[...], preferred_element_type=F32)
-        place = lax.broadcasted_iota(jnp.int32, update.shape, 0)
-        live = (place % width < length) & (first + place // width < length)
-        middle = before.astype(F32) + jnp.where(live, update, 0.0)
-        return middle.astype(BF16)
+        made = []
+        for r, row in enumerate(first):
+            at = slice(r * width, (r + 1) * width)
+            place = lax.broadcasted_iota(jnp.int32, (width, chans), 0)
+            live = (place < length) & (row < length)
+            middle = before[at].astype(F32) + jnp.where(live, update[at], 0.0)
+            made.append(middle.astype(BF16))
+        return jnp.concatenate(made, 0)
 
     def finish(middle):
         middle = middle.astype(F32)
@@ -160,13 +171,13 @@
         return (middle + down).astype(BF16)
 
     def store(i, updated):
-        out_ref[i] = updated.reshape(rows, width, chans)
+        out_ref[pl.ds(i * per, per)] = updated.reshape(per, rows, width, chans)
 
     def attend(i, slot, first):
         past = mid_s[...]
-        query, keys, side, gate = project(n_s[slot].reshape(rows * width, chans))
+        query, keys, side, gate = project(n_s[slot].reshape(span, chans))
         ends = []
-        for r in range(rows):
+        for r in range(per * rows):
             at = slice(r * width, (r + 1) * width)
             both = None
             for h in range(heads):
@@ -176,23 +187,27 @@
             ends.append(both)
         gated = gated_of(jnp.concatenate(ends, 0), gate)
         store(jnp.maximum(i - 1, 0), finish(past))
-        mid_s[...] = close(x_s[slot].reshape(rows * width, chans), first, gated)
+        mid_s[...] = close(
+            x_s[slot].reshape(span, chans), [f + r for f in first for r in range(rows)], gated
+        )
         low = functools.reduce(jnp.minimum, [e[:, inner:] for e in ends])
         high = functools.reduce(jnp.maximum, [e[:, inner:] for e in ends])
         low_s[...] = jnp.minimum(low_s[...], jnp.min(low.reshape(-1, 8, inner), 0))
         high_s[...] = jnp.maximum(high_s[...], jnp.max(high.reshape(-1, 8, inner), 0))
 
+    for copy in fetches(0, 0):
+        copy.start()
+    for h in range(heads):
+        bias_s[h] = jnp.where(keys_live, bias_ref[h].astype(F32) * LOG2E, DEAD)
     low_s[...] = jnp.ones_like(low_s)
     high_s[...] = jnp.ones_like(high_s)
     mid_s[...] = jnp.zeros_like(mid_s)
-    for copy in fetches(0, 0):
-        copy.start()
-
     def one_block(i, carry):
         slot = lax.rem(i, 2)
-        first = row_base + order_s[i] * rows
-
-        @pl.when(i + 1 < count)
+        first = firsts(i)
+        some = functools.reduce(jnp.minimum, first) < length
+
+        @pl.when(i + 1 < steps)
         def _():
             for copy in fetches(i + 1, 1 - slot):
                 copy.start()
@@ -200,58 +215,57 @@
         for copy in fetches(i, slot):
             copy.wait()
 
-        @pl.when(first < length)
+        @pl.when(some)
         def _():
             attend(i, slot, first)
 
-        @pl.when(first >= length)
+        @pl.when(jnp.logical_not(some))
         def _():
             store(jnp.maximum(i - 1, 0), finish(mid_s[...]))
-            mid_s[...] = x_s[slot].reshape(rows * width, chans)
+            mid_s[...] = x_s[slot].reshape(span, chans)
 
         return carry
 
-    lax.fori_loop(0, count, one_block, 0)
-    store(count - 1, finish(mid_s[...]))
+    lax.fori_loop(0, steps, one_block, 0)
+    store(steps - 1, finish(mid_s[...]))
     good = (jnp.min(low_s[...]) > 1e-20) & (jnp.max(high_s[...]) < 1e30)
 
     @pl.when(jnp.logical_not(good))
     def _():
         def again(i, carry):
-            first = row_base + order_s[i] * rows
-
-            @pl.when(first < length)
-            def _():
-                for copy in fetches(i, 0):
-                    copy.start()
-                for copy in fetches(i, 0):
-                    copy.wait()
-
-                def one_row(r, carry):
-                    query, keys, side, gate = project(n_s[0, r])
-
-                    def one_head(h, carry):
-                        mask = head_mask(h)
-                        score = score_of(query, keys, mask, h)
-                        each = weigh(score - jnp.max(score, -1, keepdims=True), side)
-                        sum_s[...] = jnp.where(jnp.concatenate([mask, mask], 1), each, sum_s[...])
-                        return carry
-
-                    lax.fori_loop(0, heads, one_head, 0)
-                    gated = gated_of(sum_s[...], gate)
-                    out_ref[i, r] = finish(close(x_s[0, r], first + r, gated))
+            for copy in fetches(i, 0):
+                copy.start()
+            for copy in fetches(i, 0):
+                copy.wait()
+
+            def one_row(r, carry):
+                p = r // rows
+                row = row_base + order_s[i * per + p] * rows + lax.rem(r, rows)
+                query, keys, side, gate = project(n_s[0, p, lax.rem(r, rows)])
+
+                def one_head(h, carry):
+                    mask = head_mask(h)
+                    score = score_of(query, keys, mask, h)
+                    each = weigh(score - jnp.max(score, -1, keepdims=True), side)
+                    sum_s[...] = jnp.where(jnp.concatenate([mask, mask], 1), each, sum_s[...])
                     return carry
 
-                lax.fori_loop(0, rows, one_row, 0)
-
+                lax.fori_loop(0, heads, one_head, 0)
+                gated = gated_of(sum_s[...], gate)
+                middle = close(x_s[0, p, lax.rem(r, rows)], [row], gated)
+                out_ref[i * per + p, lax.rem(r, rows)] = finish(middle)
+                return carry
+
+            lax.fori_loop(0, per * rows, one_row, 0)
             return carry
 
-        lax.fori_loop(0, count, again, 0)
+        lax.fori_loop(0, steps, again, 0)
 
 
 def update_blocks(groups, lengths, info, blocks, normeds, bias, w_proj, w_out, w_up, w_down):
     count, rows, width, chans = blocks.shape
     inner = w_proj.shape[1] // 4
+    per = 2
     vmem = pl.BlockSpec(memory_space=pltpu.VMEM)
     smem = pl.BlockSpec(memory_space=pltpu.SMEM)
     hbm = pl.BlockSpec(memory_space=pltpu.HBM)
@@ -263,15 +277,16 @@
         out_shape=jax.ShapeDtypeStruct((count, rows, width, chans), BF16),
         scratch_shapes=[
             pltpu.SMEM((count,), jnp.int32),
-            pltpu.VMEM((2, rows, width, chans), BF16),
-            pltpu.VMEM((2, rows, width, chans), BF16),
-            pltpu.VMEM((rows * width, chans), BF16),
+            pltpu.VMEM(bias.shape, F32),
+            pltpu.VMEM((2, per, rows, width, chans), BF16),
+            pltpu.VMEM((2, per, rows, width, chans), BF16),
+            pltpu.VMEM((per * rows * width, chans), BF16),
             pltpu.VMEM((width, 2 * inner), F32),
             pltpu.VMEM((8, inner), F32),
             pltpu.VMEM((8, inner), F32),
-            pltpu.SemaphoreType.DMA((2, 2)),
+            pltpu.SemaphoreType.DMA((2, per, 2)),
         ],
-        compiler_params=pltpu.CompilerParams(vmem_limit_bytes=24 * 1024 * 1024),
+        compiler_params=pltpu.CompilerParams(vmem_limit_bytes=56 * 1024 * 1024),
     )(groups, lengths, info, blocks, normeds, bias, w_proj, w_out, w_up, w_down)
 
 
@@ -284,8 +299,7 @@
     local = pair[0]
     info = jnp.stack([group_idx, axial_idx * ax_rows]).astype(jnp.int32)
     normed, bias = local_bias(local, w_bias)
-    length = jnp.take(lengths, group_idx)
-    crop_bias = masked_bias(lax.all_gather(bias, "axial", axis=1, tiled=True), length)
+    crop_bias = lax.all_gather(bias, "axial", axis=1, tiled=True)
     shape = (groups_n, blk_rows, width, chans)
     updated = update_blocks(
         block_group,

time: 326 us -> 312 us (0.957)
  local copies, waits for them, and re-layouts: 12.7 us -> 3.29 us
  Pallas kernels: 239 us -> 233 us
    unnamed x21 -> x1, local copies, waits for them, and re-layouts: 10.6 us -> 2.01 us
    pallas_call x1, Pallas kernels: 231 us -> 222 us  [update_blocks(): pl.pallas_call(update_kernel, name='update', in_specs=[smem, smem, smem,...]
where the time goes in v4:
time: 312 us
  Pallas kernels  233 us (75%)
  blocking collectives  75.3 us (24%)
  local copies, waits for them, and re-layouts  3.29 us (1%)
    pallas_call x1, Pallas kernels, update_blocks(): pl.pallas_call(update_kernel, name='update', in_specs=[smem, smem, smem,...  222 us
    all_to_all x1, blocking collectives, shards(): lax.all_to_all(updated, 'sample', split_axis=0, concat_axis=0, tiled=True)  61 us
    all_gather x1, blocking collectives, shards(): crop_bias = lax.all_gather(bias, 'axial', axis=1, tiled=True)  14.3 us
    pallas_call x1, Pallas kernels, local_bias(): pl.pallas_call(bias_kernel, name='bias', in_specs=[hbm, vmem], out_specs=...  10.5 us

profile of v4, /device:TPU:1, one launch (start us, length us, event | category | flops | bytes accessed | tf_op | source)
XLA Modules:
  0.0 311.8 jit_solution(2775082858060177859)
XLA Ops:
  0.0 1.3 pad.4.wb_ref
  1.3 10.5 %bias.1 = (bf16[64,256,128]{2,1,0:T(8,128)(2,1)}, bf16[4,64,256]{2,1,0:T(8,128)(2,1)}) custom-call(bf16[64,256,128]{2,1,0:T(8,128)(2,1)} %bitcast.8, bf16[8,128]{1,0:T(8,128)(2,1)} %pad.4.wb_ref), custom_call_target="tpu_custom_call" | custom-call | tf_op jit(solution)/shard_map/bias/pallas_call | solution.py:59
  11.8 14.3 %all_gather.3.bias_ref = bf16[4,256,256]{2,1,0:T(8,128)(2,1)} all-gather(bf16[4,64,256]{2,1,0:T(8,128)(2,1)} %get-tuple-element.8), channel_id=1, replica_groups=mesh['sample'=32,'axial'=4] {'axial'}, dimensions={1}, use_global_device_ids=true | all-gather | bytes 655360 | tf_op jit(solution)/shard_map/all_gather | solution.py:302
  26.1 0.7 pad_add_fusion.info_ref
  26.7 222.1 %update.1 = bf16[32,2,256,128]{3,2,1,0:T(8,128)(2,1)} custom-call(s32[32,32]{1,0:T(8,128)} %groups_ref.1, s32[32]{0:T(128)} %lengths_ref.1, s32[2]{0:T(128)} %pad_add_fusion.info_ref, bf16[32,2,256,128]{3,2,1,0:T(8,128)(2,1)} %bitcast.9, bf16[32,2,256,128]{3,2,1,0:T(8,128)(2,1)} %bitcast.10, bf16[4,256,256]{2,1,0:T(8,128)(2,1)} %all_gather.3.bias_ref, ...), custom_call_target="tpu_custom_call" | custom-call | tf_op jit(solution)/shard_map/update/pallas_call | solution.py:272
  248.8 61.0 %all_to_all.5 = bf16[32,2,256,128]{3,2,1,0:T(8,128)(2,1)S(1)} all-to-all(bf16[32,2,256,128]{3,2,1,0:T(8,128)(2,1)} %update.1), channel_id=1, replica_groups=mesh['sample'=32,'axial'=4] {'sample'}, dimensions={0} | all-to-all | bytes 8388608 | tf_op jit(solution)/shard_map/all_to_all | solution.py:316
  309.8 2.0 copy.10

commit v5 on v4

--- a/solution.py
+++ b/solution.py
@@ -36,16 +36,23 @@
 
     for p in range(parts):
         fetch(p).start()
-    for p in range(parts):
+
+    def one_part(p, carry):
         fetch(p).wait()
-        for r in range(p * span, (p + 1) * span):
-            normed = normalise(x_ref[r].astype(F32)).astype(BF16)
-            normed_ref[r] = normed
+        for r in range(span):
+            row = p * span + r
+            normed = normalise(x_ref[row].astype(F32)).astype(BF16)
+            normed_ref[row] = normed
             res = lax.dot_general(wb_ref[...], normed, NT, preferred_element_type=F32)
             for h in range(heads):
-                hold_ref[h, r : r + 1, :] = res[h : h + 1]
+                hold_ref[p, h, r : r + 1, :] = res[h : h + 1]
         store(p).start()
-    bias_ref[...] = hold_ref[...].astype(BF16)
+        return carry
+
+    lax.fori_loop(0, parts, one_part, 0)
+    for p in range(0, parts, 2):
+        pair = jnp.concatenate([hold_ref[p], hold_ref[p + 1]], 1)
+        bias_ref[:, p * span : (p + 2) * span, :] = pair.astype(BF16)
     for p in range(parts):
         store(p).wait()
 
@@ -68,7 +75,7 @@
         scratch_shapes=[
             pltpu.VMEM((rows, width, chans), BF16),
             pltpu.VMEM((rows, width, chans), BF16),
-            pltpu.VMEM((heads, rows, width), F32),
+            pltpu.VMEM((8, heads, rows // 8, width), F32),
             pltpu.SemaphoreType.DMA((8,)),
             pltpu.SemaphoreType.DMA((8,)),
         ],
@@ -136,14 +143,14 @@
 
     def project(normed):
         proj = jnp.dot(normed, wp_ref[...], preferred_element_type=F32)
-        query = (proj[:, :inner] * (size_h ** (-0.5) * LOG2E)).astype(BF16)
+        query = (proj[:, :inner] * size_h ** (-0.5)).astype(BF16)
         keys = proj[:, inner : 2 * inner].astype(BF16)
         values = proj[:, 2 * inner : 3 * inner].astype(BF16)
         return query, keys, jnp.concatenate([values, jnp.ones_like(values)], 1), proj[:, 3 * inner :]
 
     def score_of(query, keys, mask, h):
         score = lax.dot_general(jnp.where(mask, query, zero), keys, NT, preferred_element_type=F32)
-        return score + bias_s[h]
+        return score * LOG2E + bias_s[h]
 
     def weigh(score, side):
         return jnp.dot(jnp.exp2(score).astype(BF16), side, preferred_element_type=F32)

time: 312 us -> 312 us (level)
  no operation moved by 1% of the time
where the time goes in v5:
time: 312 us
  Pallas kernels  233 us (75%)
  blocking collectives  75.3 us (24%)
  local copies, waits for them, and re-layouts  3.29 us (1%)
    pallas_call x1, Pallas kernels, update_blocks(): pl.pallas_call(update_kernel, name='update', in_specs=[smem, smem, smem,...  222 us
    all_to_all x1, blocking collectives, shards(): lax.all_to_all(updated, 'sample', split_axis=0, concat_axis=0, tiled=True)  61 us
    all_gather x1, blocking collectives, shards(): crop_bias = lax.all_gather(bias, 'axial', axis=1, tiled=True)  14.3 us
    pallas_call x1, Pallas kernels, local_bias(): pl.pallas_call(bias_kernel, name='bias', in_specs=[hbm, vmem], out_specs=...  10.5 us

profile of v5, /device:TPU:1, one launch (start us, length us, event | category | flops | bytes accessed | tf_op | source)
XLA Modules:
  0.0 311.8 jit_solution(8309963482799149697)
XLA Ops:
  0.0 1.3 pad.4.wb_ref
  1.3 10.5 %bias.1 = (bf16[64,256,128]{2,1,0:T(8,128)(2,1)}, bf16[4,64,256]{2,1,0:T(8,128)(2,1)}) custom-call(bf16[64,256,128]{2,1,0:T(8,128)(2,1)} %bitcast.8, bf16[8,128]{1,0:T(8,128)(2,1)} %pad.4.wb_ref), custom_call_target="tpu_custom_call" | custom-call | tf_op jit(solution)/shard_map/bias/pallas_call | solution.py:66
  11.8 14.3 %all_gather.3.bias_ref = bf16[4,256,256]{2,1,0:T(8,128)(2,1)} all-gather(bf16[4,64,256]{2,1,0:T(8,128)(2,1)} %get-tuple-element.8), channel_id=1, replica_groups=mesh['sample'=32,'axial'=4] {'axial'}, dimensions={1}, use_global_device_ids=true | all-gather | bytes 655360 | tf_op jit(solution)/shard_map/all_gather | solution.py:309
  26.1 0.7 pad_add_fusion.info_ref
  26.7 222.1 %update.1 = bf16[32,2,256,128]{3,2,1,0:T(8,128)(2,1)} custom-call(s32[32,32]{1,0:T(8,128)} %groups_ref.1, s32[32]{0:T(128)} %lengths_ref.1, s32[2]{0:T(128)} %pad_add_fusion.info_ref, bf16[32,2,256,128]{3,2,1,0:T(8,128)(2,1)} %bitcast.9, bf16[32,2,256,128]{3,2,1,0:T(8,128)(2,1)} %bitcast.10, bf16[4,256,256]{2,1,0:T(8,128)(2,1)} %all_gather.3.bias_ref, ...), custom_call_target="tpu_custom_call" | custom-call | tf_op jit(solution)/shard_map/update/pallas_call | solution.py:279
  248.8 61.0 %all_to_all.5 = bf16[32,2,256,128]{3,2,1,0:T(8,128)(2,1)S(1)} all-to-all(bf16[32,2,256,128]{3,2,1,0:T(8,128)(2,1)} %update.1), channel_id=1, replica_groups=mesh['sample'=32,'axial'=4] {'sample'}, dimensions={0} | all-to-all | bytes 8388608 | tf_op jit(solution)/shard_map/all_to_all | solution.py:323
  309.8 2.0 copy.10

commit v6 on v5

--- a/solution.py
+++ b/solution.py
@@ -34,10 +34,15 @@
         part = pl.ds(p * span, span)
         return pltpu.make_async_copy(normed_ref.at[part], normed_hbm.at[part], out_sems.at[p])
 
-    for p in range(parts):
+    ahead = 2
+    for p in range(ahead):
         fetch(p).start()
 
     def one_part(p, carry):
+        @pl.when(p + ahead < parts)
+        def _():
+            fetch(p + ahead).start()
+
         fetch(p).wait()
         for r in range(span):
             row = p * span + r

time: 312 us -> 312 us (level)
  no operation moved by 1% of the time
where the time goes in v6:
time: 312 us
  Pallas kernels  233 us (75%)
  blocking collectives  75.3 us (24%)
  local copies, waits for them, and re-layouts  3.29 us (1%)
    pallas_call x1, Pallas kernels, update_blocks(): pl.pallas_call(update_kernel, name='update', in_specs=[smem, smem, smem,...  222 us
    all_to_all x1, blocking collectives, shards(): lax.all_to_all(updated, 'sample', split_axis=0, concat_axis=0, tiled=True)  61 us
    all_gather x1, blocking collectives, shards(): crop_bias = lax.all_gather(bias, 'axial', axis=1, tiled=True)  14.3 us
    pallas_call x1, Pallas kernels, local_bias(): pl.pallas_call(bias_kernel, name='bias', in_specs=[hbm, vmem], out_specs=...  10.5 us

profile of v6, /device:TPU:1, one launch (start us, length us, event | category | flops | bytes accessed | tf_op | source)
XLA Modules:
  0.0 311.8 jit_solution(11616138874519817272)
XLA Ops:
  0.0 1.3 pad.4.wb_ref
  1.3 10.5 %bias.1 = (bf16[64,256,128]{2,1,0:T(8,128)(2,1)}, bf16[4,64,256]{2,1,0:T(8,128)(2,1)}) custom-call(bf16[64,256,128]{2,1,0:T(8,128)(2,1)} %bitcast.8, bf16[8,128]{1,0:T(8,128)(2,1)} %pad.4.wb_ref), custom_call_target="tpu_custom_call" | custom-call | tf_op jit(solution)/shard_map/bias/pallas_call | solution.py:71
  11.8 14.3 %all_gather.3.bias_ref = bf16[4,256,256]{2,1,0:T(8,128)(2,1)} all-gather(bf16[4,64,256]{2,1,0:T(8,128)(2,1)} %get-tuple-element.8), channel_id=1, replica_groups=mesh['sample'=32,'axial'=4] {'axial'}, dimensions={1}, use_global_device_ids=true | all-gather | bytes 655360 | tf_op jit(solution)/shard_map/all_gather | solution.py:314
  26.1 0.7 pad_add_fusion.info_ref
  26.7 222.1 %update.1 = bf16[32,2,256,128]{3,2,1,0:T(8,128)(2,1)} custom-call(s32[32,32]{1,0:T(8,128)} %groups_ref.1, s32[32]{0:T(128)} %lengths_ref.1, s32[2]{0:T(128)} %pad_add_fusion.info_ref, bf16[32,2,256,128]{3,2,1,0:T(8,128)(2,1)} %bitcast.9, bf16[32,2,256,128]{3,2,1,0:T(8,128)(2,1)} %bitcast.10, bf16[4,256,256]{2,1,0:T(8,128)(2,1)} %all_gather.3.bias_ref, ...), custom_call_target="tpu_custom_call" | custom-call | tf_op jit(solution)/shard_map/update/pallas_call | solution.py:284
  248.8 61.0 %all_to_all.5 = bf16[32,2,256,128]{3,2,1,0:T(8,128)(2,1)S(1)} all-to-all(bf16[32,2,256,128]{3,2,1,0:T(8,128)(2,1)} %update.1), channel_id=1, replica_groups=mesh['sample'=32,'axial'=4] {'sample'}, dimensions={0} | all-to-all | bytes 8388608 | tf_op jit(solution)/shard_map/all_to_all | solution.py:328
  309.8 2.0 copy.10
